TPU v7x, 128 devices: a whole 4x4x4 slice. The times are simulated.
128 devices in a mesh: row: 16 (over y_lo, z, core), col: 8 (over y_hi, x).
Axes of the slice: x: 4, y: 4 (y_hi: 2, y_lo: 2; y = y_hi * 2 + y_lo), z: 4, core: 2. Of those that a mesh axis runs over, the one named last changes fastest.
Arguments:
- inputs: bfloat16 [2048, 12288], P('row', 'col'), may hold values from -7 to 7
- w_qkv: bfloat16 [12288, 48, 384], P('col', 'row'), may hold values from -1 to 1
- w_out: bfloat16 [48, 128, 12288], P('row', None, 'col'), may hold values from -0.078125 to 0.078125
- grad_block: bfloat16 [2048, 12288], P('row', 'col'), may hold values from -3 to 3
Outputs:
- block_out: bfloat16 [2048, 12288], P('row', 'col')
- grad_qkv: float32 [12288, 48, 384], P('col', 'row')
- grad_out: float32 [48, 128, 12288], P('row', None, 'col')
All inputs are finite; a program needn't handle non-finite values.
Results may differ from a plain program's by a relative error of at most 0.04.
Values may be sent and summed in bfloat16 or wider, within the bound.
A program may use at most 128 MiB of HBM per device.

v0:
```python
import jax
import jax.numpy as jnp
from jax import lax
from jax.sharding import PartitionSpec as P

masked_fill = -1e30


def gather_tokens(values):
    return lax.all_gather(values, "row", axis=0, tiled=True)


def gather_heads(stacked):
    return lax.all_gather(stacked, "col", axis=1, tiled=True)


def feature_sums(term, rows_here):
    return lax.psum_scatter(
        term(jnp.int32(0), lax.axis_size("col") * rows_here).astype(jnp.bfloat16),
        "col",
        scatter_dimension=0,
        tiled=True,
    ).astype(jnp.float32)


def local(inputs, w_qkv, w_out, grad_block):
    feat_cols = inputs.shape[1]
    heads_here = w_qkv.shape[1]
    head_dim = w_out.shape[1]
    local_width = heads_here * head_dim
    scale_factor = head_dim ** (-0.5)
    qkv_weight = w_qkv.reshape(feat_cols, heads_here * 3 * head_dim)
    out_weight = w_out.reshape(local_width, feat_cols)
    inputs_all = gather_tokens(inputs)
    seq_len = inputs_all.shape[0]
    query_count = seq_len // lax.axis_size("col")

    def qkv_term(first_row, row_count):
        return jnp.dot(inputs_all, qkv_weight, preferred_element_type=jnp.float32)

    qkv = (
        feature_sums(qkv_term, query_count)
        .astype(jnp.bfloat16)
        .reshape(query_count, heads_here, 3, head_dim)
    )
    queries = qkv[:, :, 0]
    key_local = qkv[:, :, 1].reshape(query_count, local_width)
    value_local = qkv[:, :, 2].reshape(query_count, local_width)
    kv_all = gather_heads(jnp.stack([key_local, value_local], axis=0))
    key_all = kv_all[0].reshape(seq_len, heads_here, head_dim)
    value_all = kv_all[1].reshape(seq_len, heads_here, head_dim)
    offset = lax.axis_index("col") * query_count
    block_rows = min(query_count, 256)
    block_count = query_count // block_rows
    key_position = jnp.arange(seq_len)
    query_blocks = queries.reshape(block_count, block_rows, heads_here, head_dim)
    block_starts = offset + block_rows * jnp.arange(block_count)

    def probability_of(query_block, first_row):
        scores = (
            jnp.einsum("qhd,khd->hqk", query_block, key_all, preferred_element_type=jnp.float32)
            * scale_factor
        )
        query_position = first_row + jnp.arange(block_rows)
        causal = key_position[None, :] <= query_position[:, None]
        scores = jnp.where(causal[None], scores, masked_fill)
        row_max = jnp.max(scores, axis=2, keepdims=True)
        exponent = jnp.exp(scores - row_max)
        return exponent / jnp.sum(exponent, axis=2, keepdims=True)

    def forward_block(operands):
        query_block, first_row = operands
        weights = probability_of(query_block, first_row).astype(jnp.bfloat16)
        return jnp.einsum(
            "hqk,khd->qhd", weights, value_all, preferred_element_type=jnp.float32
        ).astype(jnp.bfloat16)

    attended = lax.map(forward_block, (query_blocks, block_starts)).reshape(
        query_count, local_width
    )
    attended_all = gather_heads(attended[None])[0]
    block_out = lax.psum_scatter(
        jnp.dot(attended_all, out_weight, preferred_element_type=jnp.float32).astype(jnp.bfloat16),
        "row",
        scatter_dimension=0,
        tiled=True,
    )
    grad_all = gather_tokens(grad_block)
    grad_out = lax.dot_general(
        attended_all, grad_all, (((0,), (0,)), ((), ())), preferred_element_type=jnp.float32
    ).reshape(heads_here, head_dim, feat_cols)

    def grad_term(first_row, row_count):
        return lax.dot_general(
            grad_all, out_weight, (((1,), (1,)), ((), ())), preferred_element_type=jnp.float32
        )

    grad_attended = (
        feature_sums(grad_term, query_count)
        .astype(jnp.bfloat16)
        .reshape(block_count, block_rows, heads_here, head_dim)
    )

    def backward_block(carry, operands):
        key_sum, value_sum = carry
        query_block, grad_rows, first_row = operands
        probability = probability_of(query_block, first_row)
        weights = probability.astype(jnp.bfloat16)
        grad_prob = jnp.einsum(
            "qhd,khd->hqk", grad_rows, value_all, preferred_element_type=jnp.float32
        )
        grad_scores = (
            probability
            * (grad_prob - jnp.sum(probability * grad_prob, axis=2, keepdims=True))
            * scale_factor
        ).astype(jnp.bfloat16)
        grad_query = jnp.einsum(
            "hqk,khd->qhd", grad_scores, key_all, preferred_element_type=jnp.float32
        ).astype(jnp.bfloat16)
        key_sum = key_sum + jnp.einsum(
            "hqk,qhd->khd", grad_scores, query_block, preferred_element_type=jnp.float32
        )
        value_sum = value_sum + jnp.einsum(
            "hqk,qhd->khd", weights, grad_rows, preferred_element_type=jnp.float32
        )
        return ((key_sum, value_sum), grad_query)

    zero_sum = jnp.zeros((seq_len, heads_here, head_dim), jnp.float32)
    (key_sum, value_sum), grad_query = lax.scan(
        backward_block, (zero_sum, zero_sum), (query_blocks, grad_attended, block_starts)
    )
    grad_query = grad_query.reshape(query_count, local_width)

    def weight_grad(grad_rows_all):
        return lax.dot_general(
            inputs_all, grad_rows_all, (((0,), (0,)), ((), ())), preferred_element_type=jnp.float32
        ).reshape(feat_cols, heads_here, head_dim)

    grad_key = lax.psum_scatter(
        key_sum.reshape(seq_len, local_width).astype(jnp.bfloat16),
        "col",
        scatter_dimension=0,
        tiled=True,
    )
    grad_value = lax.psum_scatter(
        value_sum.reshape(seq_len, local_width).astype(jnp.bfloat16),
        "col",
        scatter_dimension=0,
        tiled=True,
    )
    all_grads = gather_heads(jnp.stack([grad_query, grad_key, grad_value], axis=0))
    grad_w_query = weight_grad(all_grads[0])
    grad_w_key = weight_grad(all_grads[1])
    grad_w_value = weight_grad(all_grads[2])
    grad_qkv = jnp.stack([grad_w_query, grad_w_key, grad_w_value], axis=2).reshape(
        feat_cols, heads_here, 3 * head_dim
    )
    return (block_out, grad_qkv, grad_out)


def solution(mesh):
    placed = (P("row", "col"), P("col", "row", None), P("row", None, "col"), P("row", "col"))
    return jax.shard_map(
        local,
        mesh=mesh,
        in_specs=placed,
        out_specs=(P("row", "col"), P("col", "row", None), P("row", None, "col")),
        check_vma=False,
    )
```

profile of v0, /device:TPU:17, one launch (start us, length us, event | category | flops | bytes accessed | tf_op | source)
XLA Modules:
  0.0 720.9 jit_solution(6494007795616689252)
XLA Ops:
  7.2 0.0 copy-start
  7.2 0.0 all-gather.6.cloned.1.call-start
  7.2 0.7 all-gather.6.cloned.1.call-update
  7.9 0.0 all-gather.12.cloned.1.call-start
  8.0 0.7 all-gather.12.cloned.1.call-update
  8.7 0.0 reduce-scatter.6.cloned.1.call-start
  8.7 6.1 copy.16
  14.8 39.9 %all-gather.6.cloned.1.call-done = bf16[2048,1536]{1,0:T(8,128)(2,1)} async-done(((bf16[128,1536]{1,0:T(8,128)(2,1)}), bf16[2048,1536]{1,0:T(8,128)(2,1)}) %all-gather.6.cloned.1.call-update) | async-done | bytes 6291472 | tf_op jit(solution)/shard_map/all_gather | solution.py:10
  54.7 12.9 %convolution_convert_fusion.1 = bf16[2048,1152]{1,0:T(8,128)(2,1)} fusion(bf16[2048,1536]{1,0:T(8,128)(2,1)} %all-gather.6.cloned.1.call-done, bf16[1536,1152]{0,1:T(8,128)(2,1)} %bitcast.93), kind=kOutput, calls=%fused_computation.3 | convolution fusion | flops 7250116608 | bytes 14548992 | tf_op jit(solution)/shard_map/dot_general | solution.py:39
  67.6 0.0 reduce-scatter.6.cloned.1.call-update
  67.6 0.0 reduce-scatter.10.cloned.1.call-start
  67.6 32.0 %all-gather.12.cloned.1.call-done = bf16[2048,1536]{1,0:T(8,128)(2,1)} async-done(((bf16[128,1536]{1,0:T(8,128)(2,1)}), bf16[2048,1536]{1,0:T(8,128)(2,1)}) %all-gather.12.cloned.1.call-update) | async-done | bytes 6291472 | tf_op jit(solution)/shard_map/all_gather | solution.py:10
  99.7 0.0 copy-done
  99.7 7.4 %convolution_convert_fusion.3 = bf16[2048,384]{1,0:T(8,128)(2,1)} fusion(bf16[2048,1536]{1,0:T(8,128)(2,1)} %all-gather.12.cloned.1.call-done, bf16[384,1536]{1,0:T(8,128)(2,1)S(1)} %bitcast.89), kind=kOutput, calls=%fused_computation.21 | convolution fusion | flops 2416705536 | bytes 9043968 | tf_op jit(solution)/shard_map/dot_general | solution.py:94
  107.0 0.0 reduce-scatter.10.cloned.1.call-update
  107.1 0.0 all-gather.8.cloned.1.call-start
  107.1 82.5 %reduce-scatter.6.cloned.1.call-done = bf16[256,1152]{1,0:T(8,128)(2,1)} async-done(((bf16[2048,1152]{1,0:T(8,128)(2,1)}), bf16[256,1152]{1,0:T(8,128)(2,1)}) %reduce-scatter.6.cloned.1.call-update) | async-done | bytes 589840 | tf_op jit(solution)/shard_map/reduce_scatter | solution.py:18
  189.6 1.3 copy.17
  190.9 0.8 pad_maximum_fusion.2
  191.7 0.0 all-gather.8.cloned.1.call-update
  191.7 0.0 reduce-scatter.14.cloned.1.call-start
  191.8 1.2 iota_compare_fusion
  193.0 75.0 %reduce-scatter.10.cloned.1.call-done = bf16[256,384]{1,0:T(8,128)(2,1)} async-done(((bf16[2048,384]{1,0:T(8,128)(2,1)}), bf16[256,384]{1,0:T(8,128)(2,1)}) %reduce-scatter.10.cloned.1.call-update) | async-done | bytes 196624 | tf_op jit(solution)/shard_map/reduce_scatter | solution.py:18
  268.0 1.1 copy.20
  269.1 67.9 %all-gather.8.cloned.1.call-done = bf16[2,2048,384]{1,2,0:T(8,128)(2,1)} async-done(((bf16[2,256,384]{1,2,0:T(8,128)(2,1)}), bf16[2,2048,384]{1,2,0:T(8,128)(2,1)}) %all-gather.8.cloned.1.call-update) | async-done | bytes 3145744 | tf_op jit(solution)/shard_map/all_gather | solution.py:14
  337.0 3.3 fusion.42
  340.3 6.6 fusion.44
  346.9 4.7 convolution_convert_fusion.2
  351.6 0.0 reduce-scatter.14.cloned.1.call-update
  351.6 0.2 reduce-scatter.12.cloned.1.call-start
  351.8 3.6 fusion.45
  355.4 14.2 %fusion.17 = bf16[3,128,2048]{2,1,0:T(8,128)(2,1)} fusion(f32[3,256,2048]{2,1,0:T(8,128)} %fusion.45, bf16[256,3,3,128]{0,3,2,1:T(8,128)(2,1)S(1)} %bitcast.99, f32[3,256,2048]{2,1,0:T(8,128)} %get-tuple-element.52, f32[3,256]{1,0:T(4,128)S(1)} %get-tuple-element.51), kind=kOutput, calls=%fused_computation.20 | convolution fusion | flops 414452480 | bytes 26943488 | tf_op jit(solution)/shard_map/while/body/eval_jaxpr/hqk,qhd->khd/dot_general | solution.py:120
  369.6 0.0 reduce-scatter.12.cloned.1.call-update
  369.6 0.0 all-gather.10.cloned.1.call-start
  369.7 4.8 fusion.27
  374.5 0.0 all-gather.10.cloned.1.call-update
  374.5 0.0 all-gather.14.cloned.1.call-start
  374.5 12.7 %fusion.30 = bf16[3,128,256]{2,1,0:T(8,128)(2,1)S(1)} fusion(bf16[2048,3,128]{0,2,1:T(8,128)(2,1)} %bitcast.103, f32[3,256,2048]{2,1,0:T(8,128)} %fusion.45, f32[3,256,2048]{2,1,0:T(8,128)} %get-tuple-element.52, f32[3,256]{1,0:T(4,128)S(1)} %get-tuple-element.51), kind=kOutput, calls=%fused_computation.34 | convolution fusion | flops 413764352 | bytes 14355456 | tf_op jit(solution)/shard_map/while/body/eval_jaxpr/hqk,khd->qhd/dot_general | solution.py:117
  387.3 37.9 %reduce-scatter.14.cloned.1.call-done = bf16[256,384]{0,1:T(8,128)(2,1)} async-done(((bf16[2048,384]{0,1:T(8,128)(2,1)}), bf16[256,384]{0,1:T(8,128)(2,1)}) %reduce-scatter.14.cloned.1.call-update) | async-done | bytes 196624 | tf_op jit(solution)/shard_map/reduce_scatter | solution.py:145
  425.2 77.3 %reduce-scatter.12.cloned.1.call-done = bf16[256,384]{0,1:T(8,128)(2,1)} async-done(((bf16[2048,384]{0,1:T(8,128)(2,1)}), bf16[256,384]{0,1:T(8,128)(2,1)}) %reduce-scatter.12.cloned.1.call-update) | async-done | bytes 196624 | tf_op jit(solution)/shard_map/reduce_scatter | solution.py:139
  502.5 1.9 pad_maximum_fusion.1
  504.4 0.0 all-gather.14.cloned.1.call-update
  504.4 0.3 reduce-scatter.8.cloned.1.call-start
  504.7 51.6 %all-gather.10.cloned.1.call-done = bf16[1,2048,384]{1,2,0:T(8,128)(2,1)} async-done(((bf16[1,256,384]{1,2,0:T(8,128)(2,1)}), bf16[1,2048,384]{1,2,0:T(8,128)(2,1)}) %all-gather.10.cloned.1.call-update) | async-done | bytes 1572880 | tf_op jit(solution)/shard_map/all_gather | solution.py:14
  556.2 6.9 convolution_convert_fusion
  563.1 0.0 copy-start.2
  563.1 0.0 reduce-scatter.8.cloned.1.call-update
  563.1 1.4 copy-done.2
  564.5 6.8 fusion.2
  571.3 70.6 %all-gather.14.cloned.1.call-done = bf16[3,2048,384]{1,2,0:T(8,128)(2,1)} async-done(((bf16[3,256,384]{1,2,0:T(8,128)(2,1)}), bf16[3,2048,384]{1,2,0:T(8,128)(2,1)}) %all-gather.14.cloned.1.call-update) | async-done | bytes 4718608 | tf_op jit(solution)/shard_map/all_gather | solution.py:14
  641.9 0.0 copy-start.1
  641.9 0.0 slice-start
  641.9 5.3 fusion.20
  647.2 0.0 copy-done.1
  647.2 0.0 slice-start.1
  647.2 4.9 fusion.21
  652.1 0.0 slice-done
  652.1 0.0 slice-done.1
  652.2 2.6 fusion.22
  654.8 3.4 pad_maximum_fusion
  658.2 8.1 %copy.27 = f32[1536,3,384]{2,0,1:T(8,128)} copy(f32[1536,3,384]{0,2,1:T(8,128)} %bitcast.90) | data formatting | bytes 14155776
  666.3 47.7 %reduce-scatter.8.cloned.1.call-done = bf16[128,1536]{1,0:T(8,128)(2,1)} async-done(((bf16[2048,1536]{1,0:T(8,128)(2,1)}), bf16[128,1536]{1,0:T(8,128)(2,1)}) %reduce-scatter.8.cloned.1.call-update) | async-done | bytes 393232 | tf_op jit(solution)/shard_map/reduce_scatter | solution.py:82
  (3 shorter events, 0.0 us)
Async XLA Ops:
  7.2 92.5 %copy-start = (bf16[3,128,1536]{2,1,0:T(8,128)(2,1)S(1)}, bf16[3,128,1536]{2,1,0:T(8,128)(2,1)}, u32[]{:S(2)}) copy-start(bf16[3,128,1536]{2,1,0:T(8,128)(2,1)} %param.6) | copy-start | bytes 3538948
  7.2 47.5 %all-gather.6.cloned.1.call-start = ((), (), s32[]{:S(2)}) async-start(), calls=%async_computation.5 | async-start | bytes 6684672 | tf_op jit(solution)/shard_map/all_gather | solution.py:10
  7.9 91.7 %all-gather.12.cloned.1.call-start = ((), (), s32[]{:S(2)}) async-start(), calls=%async_computation.10 | async-start | bytes 6684672 | tf_op jit(solution)/shard_map/all_gather | solution.py:10
  8.7 180.9 %reduce-scatter.6.cloned.1.call-start = ((), (), s32[]{:S(2)}) async-start(), calls=%async_computation.6 | async-start | bytes 5308416 | tf_op jit(solution)/shard_map/reduce_scatter | solution.py:18
  67.6 200.5 %reduce-scatter.10.cloned.1.call-start = ((), (), s32[]{:S(2)}) async-start(), calls=%async_computation.11 | async-start | bytes 1769472 | tf_op jit(solution)/shard_map/reduce_scatter | solution.py:18
  107.1 229.9 %all-gather.8.cloned.1.call-start = ((), (), s32[]{:S(2)}) async-start(), calls=%async_computation.7 | async-start | bytes 3538944 | tf_op jit(solution)/shard_map/all_gather | solution.py:14
  191.7 233.4 %reduce-scatter.14.cloned.1.call-start = ((), (), s32[]{:S(2)}) async-start(), calls=%async_computation.13 | async-start | bytes 1769472 | tf_op jit(solution)/shard_map/reduce_scatter | solution.py:145
  351.6 150.9 %reduce-scatter.12.cloned.1.call-start = ((), (), s32[]{:S(2)}) async-start(), calls=%async_computation.12 | async-start | bytes 1769472 | tf_op jit(solution)/shard_map/reduce_scatter | solution.py:139
  369.6 186.6 %all-gather.10.cloned.1.call-start = ((), (), s32[]{:S(2)}) async-start(), calls=%async_computation.8 | async-start | bytes 1769472 | tf_op jit(solution)/shard_map/all_gather | solution.py:14
  374.5 267.4 %all-gather.14.cloned.1.call-start = ((), (), s32[]{:S(2)}) async-start(), calls=%async_computation.14 | async-start | bytes 5308416 | tf_op jit(solution)/shard_map/all_gather | solution.py:14
  504.4 209.7 %reduce-scatter.8.cloned.1.call-start = ((), (), s32[]{:S(2)}) async-start(), calls=%async_computation.9 | async-start | bytes 6684672 | tf_op jit(solution)/shard_map/reduce_scatter | solution.py:82
  563.1 1.4 copy-start.2
  641.9 5.3 copy-start.1
  641.9 10.2 %slice-start = ((s8[6291456]{0:T(1024)(128)(4,1)}), s8[4194304]{0:T(1024)(128)(4,1)S(1)}, s32[]{:S(2)}) async-start(s8[6291456]{0:T(1024)(128)(4,1)} %bitcast.112), calls=%async_computation.15 | async-start | bytes 8388608
  647.2 4.9 slice-start.1
Sparse Core Ops, SparseCore 0:
  9.7 44.8 all-gather.5
  56.4 43.2 all-gather.11
  104.2 85.3 reduce-scatter.5
  194.3 73.7 reduce-scatter.9
  270.9 66.0 all-gather.7
  351.7 73.3 reduce-scatter.13
  429.4 73.0 reduce-scatter.11
  505.4 50.7 all-gather.9
  559.2 82.6 all-gather.13
  644.9 69.1 reduce-scatter.7
where the time goes:
time: 726 us; the launch traced here: 721 us
  waiting for transfers between devices  584 us (80%)
  matrix products  93.3 us (13%)
  local copies, waits for them, and re-layouts  21.3 us (3%)
  between operations  14.3 us (2%)
  other arithmetic  7.33 us (1%)
    all_gather x3, waiting for transfers between devices, gather_heads(): return lax.all_gather(stacked, 'col', axis=1, tiled=True)  190 us
    reduce_scatter x2, waiting for transfers between devices, feature_sums(): lax.psum_scatter(term(jnp.int32(0), lax.axis_size('col') * rows_here).ast...  158 us
    reduce_scatter x1, waiting for transfers between devices, local(): lax.psum_scatter(key_sum.reshape(seq_len, local_width).astype(jnp.bfloat1...  77.3 us
    all_gather x2, waiting for transfers between devices, gather_tokens(): return lax.all_gather(values, 'row', axis=0, tiled=True)  71.9 us
    reduce_scatter x1, waiting for transfers between devices, local(): lax.psum_scatter(jnp.dot(attended_all, out_weight, preferred_element_type...  47.7 us
    reduce_scatter x1, waiting for transfers between devices, local(): lax.psum_scatter(value_sum.reshape(seq_len, local_width).astype(jnp.bfloa...  37.9 us
    unnamed x12, local copies, waits for them, and re-layouts  15.6 us
  transfers between devices with their start and end apart: 10, of which 10 were waited for; matrix products, arithmetic and copies ran while one was open for 15% of the time, Pallas kernels for 0%

commit v1 on v0

v1 whole, which is shorter than its diff:
```python
import jax
import jax.numpy as jnp
from jax import lax
from jax.experimental import pallas as pl
from jax.experimental.pallas import tpu as pltpu
from jax.sharding import PartitionSpec as P

MESH = pl.DeviceIdType.MESH
BF16 = jnp.bfloat16
F32 = jnp.float32


class Place:
    def __init__(self):
        r = lax.axis_index("row")
        c = lax.axis_index("col")
        self.ylo, self.z, self.core = r // 8, (r // 2) % 4, r % 2
        self.yhi, self.x = c // 4, c % 4

    def at(self, ylo=0, z=0, core=0, yhi=0, x=0):
        return (
            lax.rem(self.ylo + ylo, 2) * 8 + lax.rem(self.z + z + 4, 4) * 2 + lax.rem(self.core + core, 2),
            lax.rem(self.yhi + yhi, 2) * 4 + lax.rem(self.x + x + 4, 4),
        )

    def slot(self, ylo=0, z=0, core=0):
        return self.at(ylo=ylo, z=z, core=core)[0]

    def col_x(self, x):
        return lax.rem(self.x + x + 4, 4)


def meet(partners):
    barrier = pltpu.get_barrier_semaphore()
    for partner in partners:
        pl.semaphore_signal(barrier, inc=1, device_id=partner, device_id_type=MESH)
    pl.semaphore_wait(barrier, len(partners))


def remote(src, dst, send, recv, device):
    return pltpu.make_async_remote_copy(
        src_ref=src, dst_ref=dst, send_sem=send, recv_sem=recv, device_id=device, device_id_type=MESH
    )


def project_kernel(
    x_ref, g_ref, w_hbm, wo_ref,
    all_out, sum_out,
    held, part, relay, near, far, mine, total, w_ref,
    ag_send, ag_recv, s1_send, s1_recv, s2_send, s2_recv, s3_send, s3_recv, s4_send, s4_recv,
    out_sem, w_sem, own_sem,
):
    me = Place()
    up, down = dict(z=1), dict(z=-1)
    own_rows = (x_ref, g_ref)
    right, left, across, twin = me.at(x=1), me.at(x=-1), me.at(yhi=1), me.at(core=1)
    is_home = me.core == me.yhi
    w_copy = pltpu.make_async_copy(w_hbm, w_ref, w_sem)
    w_copy.start()
    own_copy = []
    for a in (0, 1):
        copy = pltpu.make_async_copy(own_rows[a], held.at[a, me.slot()], own_sem.at[a])
        copy.start()
        own_copy.append(copy)
    meet([me.at(ylo=1), me.at(**up), me.at(**down), twin, right, left, across])

    def gather(a, k):
        whole = pl.ds(0, 128)
        first, second = pl.ds(0, 64), pl.ds(64, 64)
        slot, rows, device = {
            0: (me.slot(), whole, me.at(ylo=1)),
            1: (me.slot(), whole, me.at(**up)),
            2: (me.slot(), whole, me.at(**down)),
            3: (me.slot(ylo=1), whole, me.at(**up)),
            4: (me.slot(ylo=1), whole, me.at(**down)),
            5: (me.slot(z=-1), first, me.at(**up)),
            6: (me.slot(z=1), second, me.at(**down)),
            7: (me.slot(ylo=1, z=-1), first, me.at(**up)),
            8: (me.slot(ylo=1, z=1), second, me.at(**down)),
            9: (me.slot(), whole, twin),
            10: (me.slot(ylo=1), whole, twin),
            11: (me.slot(z=-1), whole, twin),
            12: (me.slot(z=1), whole, twin),
            13: (me.slot(ylo=1, z=-1), whole, twin),
            14: (me.slot(ylo=1, z=1), whole, twin),
            15: (me.slot(z=2), whole, twin),
            16: (me.slot(ylo=1, z=2), whole, twin),
        }[k]
        ref = held.at[a, slot, rows]
        src = own_rows[a] if k in (0, 1, 2, 9) else ref
        return remote(src, ref, ag_send.at[a, k], ag_recv.at[a, k], device)

    def go(a, *kinds):
        for k in kinds:
            gather(a, k).start()

    def landed(a, *kinds):
        for k in kinds:
            gather(a, k).wait_recv()

    def block_of(s):
        ylo = jnp.where((s == 1) | (s == 4) | (s == 5) | (s == 7), 1, 0)
        z = jnp.where((s == 2) | (s == 4), 3, jnp.where((s == 3) | (s == 5), 1, jnp.where(s >= 6, 2, 0)))
        return lax.rem(me.ylo + ylo, 2) * 4 + lax.rem(me.z + z, 4)

    def unit(a):
        return pl.ds(0, 3) if a == 0 else pl.ds(3, 1)

    def keep(a, s):
        pair = pl.ds(block_of(s) * 2, 2)
        return pltpu.make_async_copy(held.at[a, pair], all_out.at[a, pair], out_sem.at[a, s])

    def rs1(a, s):
        start = me.col_x(2) * 64
        return [
            remote(part.at[s, unit(a), pl.ds(pl.multiple_of(start + 32 * d, 32), 32)], relay.at[s, d, unit(a)],
                   s1_send.at[a, s, d], s1_recv.at[a, s, d], (right, left)[d])
            for d in (0, 1)
        ]

    def rs2(a, s):
        return [
            remote(part.at[s, unit(a), pl.ds(pl.multiple_of(me.col_x((1, -1)[d]) * 64, 64), 64)], near.at[s, d, unit(a)],
                   s2_send.at[a, s, d], s2_recv.at[a, s, d], (right, left)[d])
            for d in (0, 1)
        ]

    def rs3(a, s):
        return remote(mine.at[s, unit(a)], far.at[s, unit(a)], s3_send.at[a, s], s3_recv.at[a, s], across)

    def rs4(a, s):
        rows = total.at[block_of(s), unit(a)]
        return remote(rows, rows, s4_send.at[a, s], s4_recv.at[a, s], twin)

    def multiply(a, s):
        rows = held.at[a, pl.ds(block_of(s) * 2, 2)]
        keep(a, s).start()
        if a == 0:
            @pl.loop(0, 3)
            def _(h):
                part[s, h] = jnp.dot(
                    rows[...].reshape(256, 1536), w_ref[h], preferred_element_type=F32
                ).astype(BF16)
        else:
            part[s, 3] = lax.dot_general(
                rows[...].reshape(256, 1536), wo_ref[...].reshape(384, 1536),
                (((1,), (1,)), ((), ())), preferred_element_type=F32,
            ).astype(BF16)
        for copy in rs1(a, s):
            copy.start()

    def each(steps, body):
        lo, hi = steps
        if hi - lo == 1:
            body(lo)
        else:
            pl.loop(lo, hi)(body)

    def work(a, *steps):
        def body(s):
            gather_twin(a, s)
            multiply(a, s)
        each(steps, body)

    def gather_twin(a, s):
        remote(held.at[a, 0], held.at[a, 0], ag_send.at[a, 9 + s], ag_recv.at[a, 9 + s], twin).wait_recv()

    def add_relay(a, *steps):
        def body(s):
            sends = rs2(a, s)
            for d in (0, 1):
                rs1(a, s)[d].wait_recv()
                rows = pl.ds(pl.multiple_of(me.col_x((1, -1)[d]) * 64 + 32 * d, 32), 32)
                part[s, unit(a), rows] = (
                    part[s, unit(a), rows].astype(F32) + relay[s, d, unit(a)].astype(F32)
                ).astype(BF16)
                sends[d].start()
        each(steps, body)

    def add_near(a, *steps):
        def body(s):
            for d in (0, 1):
                rs2(a, s)[d].wait_recv()
            rows = pl.ds(pl.multiple_of(me.x * 64, 64), 64)
            mine[s, unit(a)] = (
                part[s, unit(a), rows].astype(F32)
                + near[s, 0, unit(a)].astype(F32)
                + near[s, 1, unit(a)].astype(F32)
            ).astype(BF16)

            @pl.when(jnp.logical_not(is_home))
            def _():
                rs3(a, s).start()
        each(steps, body)

    def add_far(a, *steps):
        @pl.when(is_home)
        def _():
            def body(s):
                rs3(a, s).wait_recv()
                total[block_of(s), unit(a)] = (
                    mine[s, unit(a)].astype(F32) + far[s, unit(a)].astype(F32)
                ).astype(BF16)
                rs4(a, s).start()
            each(steps, body)

    go(0, 9, 0, 1, 2)
    go(1, 9)
    w_copy.wait()
    for copy in own_copy:
        copy.wait()
    work(0, 0, 1)
    work(1, 0, 1)
    landed(0, 0)
    go(0, 3, 4, 10)
    go(1, 0)
    landed(0, 1)
    go(0, 5, 11)
    landed(0, 2)
    go(0, 6, 12)
    work(0, 1, 4)
    add_relay(0, 0, 1)
    add_relay(1, 0, 1)
    add_relay(0, 1, 2)
    landed(0, 3)
    go(0, 7, 13)
    landed(0, 4)
    go(0, 8, 14)
    go(1, 1, 2)
    work(0, 4, 6)
    add_near(0, 0, 1)
    add_near(1, 0, 1)
    add_relay(0, 2, 4)
    landed(0, 5, 6)
    go(0, 15)
    landed(1, 0)
    go(1, 3, 4, 10)
    landed(0, 7, 8)
    go(0, 16)
    work(0, 6, 8)
    work(1, 1, 2)
    add_near(0, 1, 4)
    add_relay(0, 4, 6)
    landed(1, 1)
    go(1, 5, 11)
    landed(1, 2)
    go(1, 6, 12)
    work(1, 2, 4)
    add_far(0, 0, 4)
    add_relay(0, 6, 8)
    add_near(0, 4, 6)
    landed(1, 3)
    go(1, 7, 13)
    landed(1, 4)
    go(1, 8, 14)
    work(1, 4, 6)
    add_relay(1, 1, 4)
    add_near(0, 6, 8)
    landed(1, 5, 6)
    go(1, 15)
    landed(1, 7, 8)
    go(1, 16)
    work(1, 6, 8)
    add_far(0, 4, 8)
    add_relay(1, 4, 6)
    add_near(1, 1, 4)
    add_relay(1, 6, 8)
    add_near(1, 4, 8)
    add_far(1, 0, 8)

    for a in (0, 1):
        @pl.when(jnp.logical_not(is_home))
        def _():
            @pl.loop(0, 8)
            def _(s):
                rs3(a, s).wait_send()
                rs4(a, s).wait_recv()

        @pl.when(is_home)
        def _():
            @pl.loop(0, 8)
            def _(s):
                rs4(a, s).wait_send()
    result = pltpu.make_async_copy(total, sum_out, w_sem)
    result.start()
    for a in (0, 1):
        for k in range(17):
            gather(a, k).wait_send()

        @pl.loop(0, 8)
        def _(s):
            keep(a, s).wait()
            for d in (0, 1):
                rs1(a, s)[d].wait_send()
                rs2(a, s)[d].wait_send()
    result.wait()


def project(inputs, grad_block, w_qkv, w_out):
    dma = pltpu.SemaphoreType.DMA
    anywhere = pl.BlockSpec(memory_space=pl.ANY)
    vmem = pl.BlockSpec(memory_space=pltpu.VMEM)
    return pl.pallas_call(
        project_kernel,
        name="project",
        out_shape=(
            jax.ShapeDtypeStruct((2, 16, 128, 1536), BF16),
            jax.ShapeDtypeStruct((8, 4, 64, 384), BF16),
        ),
        in_specs=[vmem, vmem, anywhere, vmem],
        out_specs=(anywhere, anywhere),
        scratch_shapes=[
            pltpu.VMEM((2, 16, 128, 1536), BF16),
            pltpu.VMEM((8, 4, 256, 384), BF16),
            pltpu.VMEM((8, 2, 4, 32, 384), BF16),
            pltpu.VMEM((8, 2, 4, 64, 384), BF16),
            pltpu.VMEM((8, 4, 64, 384), BF16),
            pltpu.VMEM((8, 4, 64, 384), BF16),
            pltpu.VMEM((8, 4, 64, 384), BF16),
            pltpu.VMEM((3, 1536, 384), BF16),
            dma((2, 17)), dma((2, 17)),
            dma((2, 8, 2)), dma((2, 8, 2)),
            dma((2, 8, 2)), dma((2, 8, 2)),
            dma((2, 8)), dma((2, 8)),
            dma((2, 8)), dma((2, 8)),
            dma((2, 8)), dma(()), dma((2,)),
        ],
        compiler_params=pltpu.CompilerParams(
            collective_id=1, has_side_effects=True, vmem_limit_bytes=60 << 20
        ),
    )(inputs, grad_block, jnp.transpose(w_qkv, (1, 0, 2)), w_out)


def attend_kernel(
    rows_ref, out,
    kv, scores, slopes, part, twin_part, relay, near, result,
    ag_send, ag_recv, tw_send, tw_recv, s1_send, s1_recv, s2_send, s2_recv, up_send, up_recv, out_sem,
):
    me = Place()
    right, left, twin = me.at(x=1), me.at(x=-1), me.at(core=1)
    is_home = me.core == me.yhi
    scale = 128 ** (-0.5)
    fill = -1e30

    def own(x=0):
        return pl.ds(pl.multiple_of(me.col_x(x) * 64, 64), 64)

    my_rows = pl.ds(pl.multiple_of(me.core * 32, 32), 32)
    low, high = pl.ds(0, 4), pl.ds(4, 4)
    every = pl.ds(0, 8)
    for h in range(3):
        for j in (0, 1):
            kv[j, h, :, own()] = rows_ref[:, h, :, 128 + 128 * j:256 + 128 * j]
    meet([twin, right, left])

    def gather(h, k):
        x, blocks, device = {
            0: (0, every, right),
            1: (0, every, left),
            2: (-1, low, right),
            3: (1, high, left),
            4: (-1, every, twin),
            5: (1, every, twin),
            6: (2, every, twin),
        }[k]
        ref = kv.at[me.core, h, blocks, own(x)]
        return remote(ref, ref, ag_send.at[h, k], ag_recv.at[h, k], device)

    def pass_on(h):
        for d in (0, 1):
            gather(h, d).wait_recv()
            gather(h, 2 + d).start()
            gather(h, 4 + d).start()

    def complete(h):
        gather(h, 2).wait_recv()
        gather(h, 3).wait_recv()
        gather(h, 6).start()
        for k in (4, 5, 6):
            gather(h, k).wait_recv()

    def attend(h):
        query = rows_ref[:, h, my_rows, 0:128].reshape(256, 128)
        cotangent = rows_ref[:, 3, my_rows, h * 128:(h + 1) * 128].reshape(256, 128)
        transposed = (((1,), (1,)), ((), ()))
        first = (((0,), (0,)), ((), ()))

        def masked(b, lanes):
            width = 256 - lanes
            s = lax.dot_general(kv[0, h, b], query[lanes:], transposed, preferred_element_type=F32) * scale
            key_at = b * 256 + lax.broadcasted_iota(jnp.int32, (256, width), 0)
            column = lanes + lax.broadcasted_iota(jnp.int32, (1, width), 1)
            query_at = (column // 32) * 256 + me.x * 64 + me.core * 32 + column % 32
            return jnp.where(key_at <= query_at, s, fill)

        def top(lanes):
            def body(b, m):
                s = masked(b, lanes)
                scores[b, :, lanes:] = s
                return jnp.maximum(m, jnp.max(s, axis=0, keepdims=True))
            return body

        m = lax.fori_loop(0, 4, top(0), jnp.full((1, 256), fill, F32))
        m_high = lax.fori_loop(4, 8, top(128), m[:, 128:])
        m = jnp.concatenate([m[:, :128], m_high], axis=1)

        def sums(lanes, m):
            def body(b, carry):
                total, slope = carry
                e = jnp.exp(scores[b, :, lanes:] - m)
                scores[b, :, lanes:] = e
                dp = lax.dot_general(kv[1, h, b], cotangent[lanes:], transposed, preferred_element_type=F32)
                slopes[b, :, lanes:] = dp
                return (total + jnp.sum(e, axis=0, keepdims=True), slope + jnp.sum(e * dp, axis=0, keepdims=True))
            return body

        zero = jnp.zeros((1, 256), F32)
        total, slope = lax.fori_loop(0, 4, sums(0, m), (zero, zero))
        total_high, slope_high = lax.fori_loop(4, 8, sums(128, m_high), (total[:, 128:], slope[:, 128:]))
        total = jnp.concatenate([total[:, :128], total_high], axis=1)
        slope = jnp.concatenate([slope[:, :128], slope_high], axis=1)
        inverse = 1.0 / total
        slope = slope * inverse

        def grads(lanes):
            def body(b, carry):
                att, dq = carry
                p = scores[b, :, lanes:] * inverse[:, lanes:]
                w = p.astype(BF16)
                ds = (p * (slopes[b, :, lanes:] - slope[:, lanes:]) * scale).astype(BF16)
                part[h, 0, b] = jnp.dot(ds, query[lanes:], preferred_element_type=F32).astype(BF16)
                part[h, 1, b] = jnp.dot(w, cotangent[lanes:], preferred_element_type=F32).astype(BF16)
                att = att + lax.dot_general(kv[1, h, b], w, first, preferred_element_type=F32)
                dq = dq + lax.dot_general(kv[0, h, b], ds, first, preferred_element_type=F32)
                return att, dq
            return body

        square = jnp.zeros((128, 256), F32)
        att, dq = lax.fori_loop(0, 4, grads(0), (square, square))
        att_high, dq_high = lax.fori_loop(4, 8, grads(128), (att[:, 128:], dq[:, 128:]))
        for t, lo, hi in ((0, att, att_high), (1, dq, dq_high)):
            rows = jnp.concatenate([lo[:, :128], hi], axis=1).T.astype(BF16)
            result[t, h, :, my_rows] = rows.reshape(8, 32, 128)

    def to_twin(h):
        return remote(part.at[h, 1 - me.core], twin_part.at[h], tw_send.at[h], tw_recv.at[h], twin)

    def lift(h, t):
        if t < 2:
            ref = result.at[t, h, every, my_rows]
        else:
            ref = result.at[2 + me.core, h]
        return remote(ref, ref, up_send.at[h, t], up_recv.at[h, t], twin)

    def after(h):
        to_twin(h).start()

        @pl.when(jnp.logical_not(is_home))
        def _():
            lift(h, 0).start()
            lift(h, 1).start()

    def rs1(h, d):
        return remote(part.at[h, me.core, (low, high)[d], own(2)], relay.at[h, d],
                      s1_send.at[h, d], s1_recv.at[h, d], (right, left)[d])

    def rs2(h, d):
        return remote(part.at[h, me.core, every, own((1, -1)[d])], near.at[h, d],
                      s2_send.at[h, d], s2_recv.at[h, d], (right, left)[d])

    def add_twin(h):
        to_twin(h).wait_recv()

        @pl.loop(0, 8)
        def _(b):
            part[h, me.core, b] = (part[h, me.core, b].astype(F32) + twin_part[h, b].astype(F32)).astype(BF16)

        for d in (0, 1):
            rs1(h, d).start()

    def add_relay(h):
        for d in (0, 1):
            rs1(h, d).wait_recv()
            here = part.at[h, me.core, (low, high)[d], own((1, -1)[d])]
            here[...] = (here[...].astype(F32) + relay[h, d].astype(F32)).astype(BF16)
            rs2(h, d).start()

    def add_near(h):
        for d in (0, 1):
            rs2(h, d).wait_recv()
        result[2 + me.core, h] = (
            part[h, me.core, :, own()].astype(F32) + near[h, 0].astype(F32) + near[h, 1].astype(F32)
        ).astype(BF16)

        @pl.when(jnp.logical_not(is_home))
        def _():
            lift(h, 2).start()

    for h in range(3):
        gather(h, 0).start()
        gather(h, 1).start()
    pass_on(0)
    pass_on(1)
    complete(0)
    attend(0)
    after(0)
    pass_on(2)
    complete(1)
    add_twin(0)
    attend(1)
    after(1)
    add_relay(0)
    complete(2)
    add_twin(1)
    attend(2)
    after(2)
    add_relay(1)
    add_near(0)
    add_twin(2)
    add_near(1)
    add_relay(2)
    add_near(2)

    @pl.when(jnp.logical_not(is_home))
    def _():
        for h in range(3):
            for t in range(3):
                lift(h, t).wait_send()

    @pl.when(is_home)
    def _():
        their_rows = pl.ds(pl.multiple_of(32 - me.core * 32, 32), 32)
        for h in range(3):
            for t in range(3):
                ref = result.at[t, h, every, their_rows] if t < 2 else result.at[3 - me.core, h]
                remote(ref, ref, up_send.at[h, t], up_recv.at[h, t], twin).wait_recv()

    copy = pltpu.make_async_copy(result, out, out_sem)
    copy.start()
    for h in range(3):
        for k in range(7):
            gather(h, k).wait_send()
        to_twin(h).wait_send()
        for d in (0, 1):
            rs1(h, d).wait_send()
            rs2(h, d).wait_send()
    copy.wait()


def attend_heads(rows):
    dma = pltpu.SemaphoreType.DMA
    return pl.pallas_call(
        attend_kernel,
        name="attend",
        out_shape=jax.ShapeDtypeStruct((4, 3, 8, 64, 128), BF16),
        in_specs=[pl.BlockSpec(memory_space=pltpu.VMEM)],
        out_specs=pl.BlockSpec(memory_space=pl.ANY),
        scratch_shapes=[
            pltpu.VMEM((2, 3, 8, 256, 128), BF16),
            pltpu.VMEM((8, 256, 256), F32),
            pltpu.VMEM((8, 256, 256), F32),
            pltpu.VMEM((3, 2, 8, 256, 128), BF16),
            pltpu.VMEM((3, 8, 256, 128), BF16),
            pltpu.VMEM((3, 2, 4, 64, 128), BF16),
            pltpu.VMEM((3, 2, 8, 64, 128), BF16),
            pltpu.VMEM((4, 3, 8, 64, 128), BF16),
            dma((3, 7)), dma((3, 7)),
            dma((3,)), dma((3,)),
            dma((3, 2)), dma((3, 2)),
            dma((3, 2)), dma((3, 2)),
            dma((3, 3)), dma((3, 3)),
            dma(()),
        ],
        compiler_params=pltpu.CompilerParams(
            collective_id=2, has_side_effects=True, vmem_limit_bytes=60 << 20
        ),
    )(rows)

slice_at = (0, -1, 1, 2)


def combine_kernel(
    all_hbm, rows_hbm, wo_ref,
    block_out, grad_qkv, grad_out,
    held, stage, turned, tokens_g, turned_a, part, twin_part, relay, near, far, final, ours, theirs,
    own_sem, x_sem, g_sem, ag_send, ag_recv, tw_send, tw_recv, s1_send, s1_recv, s2_send, s2_recv, s3_send, s3_recv, end_send, end_recv,
):
    me = Place()
    right, left, across, twin = me.at(x=1), me.at(x=-1), me.at(yhi=1), me.at(core=1)
    up, down, beside = me.at(z=1), me.at(z=-1), me.at(ylo=1)
    is_home = me.core == me.yhi
    low, high, every = pl.ds(0, 4), pl.ds(4, 4), pl.ds(0, 8)

    def rows(i):
        return pl.ds(pl.multiple_of(me.col_x(slice_at[i]) * 64, 64), 64)

    def load_x(i):
        return pltpu.make_async_copy(all_hbm.at[0, every, rows(i)], stage.at[i % 2], x_sem.at[i])

    def load_g(i):
        return pltpu.make_async_copy(all_hbm.at[1, every, rows(i)], tokens_g.at[i], g_sem.at[i])

    def load_own(t):
        return pltpu.make_async_copy(rows_hbm.at[t], held.at[t, :, every, rows(0)], own_sem.at[t])

    @pl.when(is_home)
    def _():
        for t in range(4):
            load_own(t).start()

    for i in range(4):
        load_g(i).start()
    load_x(0).start()
    load_x(1).start()
    meet([right, left, across, twin, up, down, beside])

    def gather(t, k):
        i, blocks, device = {
            0: (0, every, across),
            1: (0, every, right),
            2: (0, every, left),
            3: (1, low, right),
            4: (2, high, left),
        }[k]
        ref = held.at[t, :, blocks, rows(i)]
        return remote(ref, ref, ag_send.at[t, k], ag_recv.at[t, k], device)

    def ready(t):
        @pl.when(is_home)
        def _():
            load_own(t).wait()
            gather(t, 0).start()

        @pl.when(jnp.logical_not(is_home))
        def _():
            gather(t, 0).wait_recv()

        gather(t, 1).start()
        gather(t, 2).start()

    def pass_on(t):
        for d in (0, 1):
            gather(t, 1 + d).wait_recv()
            gather(t, 3 + d).start()

    def complete(t):
        gather(t, 3).wait_recv()
        gather(t, 4).wait_recv()

    def turn(i):
        load_x(i).wait()

        @pl.loop(0, 12)
        def _(n):
            lanes = pl.ds(pl.multiple_of(n * 128, 128), 128)
            turned[i, lanes] = stage[i % 2, :, :, lanes].reshape(512, 128).T

        if i < 2:
            load_x(i + 2).start()

    def to_twin(i):
        return remote(part.at[i, 1 - me.core], twin_part.at[i], tw_send.at[i], tw_recv.at[i], twin)

    def multiply_out(i):
        mine = jnp.concatenate([held[0, h, :, rows(i)].reshape(512, 128) for h in range(3)], axis=1)
        turned_a[...] = mine.T
        load_g(i).wait()

        @pl.loop(0, 2)
        def _(j):
            @pl.loop(0, 2)
            def _(n):
                lanes = pl.ds(pl.multiple_of(j * 768 + n * 384, 384), 384)
                inner = pl.ds(pl.multiple_of(n * 384, 384), 384)
                part[i, j, :, :, :, inner] = jnp.dot(
                    mine, wo_ref[:, :, lanes].reshape(384, 384), preferred_element_type=F32
                ).astype(BF16).reshape(2, 4, 64, 384)

        to_twin(i).start()

        @pl.loop(0, 4)
        def _(n):
            lanes = pl.ds(pl.multiple_of(n * 384, 384), 384)
            term = jnp.dot(
                turned_a[...], tokens_g[i, :, :, lanes].reshape(512, 384), preferred_element_type=F32
            ).reshape(3, 128, 384)
            if i == 0:
                grad_out[:, :, lanes] = term
            else:
                grad_out[:, :, lanes] += term

    def multiply_grads(i):
        @pl.loop(0, 3)
        def _(h):
            grads = jnp.concatenate([held[t, h, :, rows(i)].reshape(512, 128) for t in (1, 2, 3)], axis=1)

            @pl.loop(0, 3)
            def _(m):
                features = pl.ds(pl.multiple_of(m * 512, 512), 512)
                term = jnp.dot(turned[i, features], grads, preferred_element_type=F32)
                if i == 0:
                    grad_qkv[h, features] = term
                else:
                    grad_qkv[h, features] += term

    def z_at(z):
        return lax.rem(me.z + z + 4, 4)

    def rs1(i, d):
        return remote(part.at[i, me.core, d, z_at(2)], relay.at[i, d], s1_send.at[i, d], s1_recv.at[i, d], (up, down)[d])

    def rs2(i, d):
        return remote(part.at[i, me.core, :, z_at((1, -1)[d])], near.at[i, d], s2_send.at[i, d], s2_recv.at[i, d], (up, down)[d])

    def rs3(i):
        return remote(part.at[i, me.core, 1 - me.ylo, me.z], far.at[i], s3_send.at[i], s3_recv.at[i], beside)

    def add(ref, *terms):
        value = ref[...].astype(F32)
        for term in terms:
            value = value + term.astype(F32)
        ref[...] = value.astype(BF16)

    def add_twin(i):
        to_twin(i).wait_recv()

        @pl.loop(0, 4)
        def _(z):
            for y in (0, 1):
                add(part.at[i, me.core, y, z], twin_part[i, y, z])

        for d in (0, 1):
            rs1(i, d).start()

    def add_relay(i):
        for d in (0, 1):
            rs1(i, d).wait_recv()
            add(part.at[i, me.core, d, z_at((1, -1)[d])], relay[i, d])
            rs2(i, d).start()

    def add_near(i):
        for d in (0, 1):
            rs2(i, d).wait_recv()
        for y in (0, 1):
            add(part.at[i, me.core, y, me.z], near[i, 0, y], near[i, 1, y])
        rs3(i).start()

    def add_far(i):
        rs3(i).wait_recv()
        final[rows(i)] = (part[i, me.core, me.ylo, me.z].astype(F32) + far[i].astype(F32)).astype(BF16)

    ready(0)
    ready(1)
    multiply_out(0)
    turn(0)
    add_twin(0)
    turn(1)
    pass_on(0)
    ready(2)
    multiply_out(1)
    multiply_out(2)
    add_relay(0)
    add_twin(1)
    add_twin(2)
    turn(2)
    pass_on(1)
    ready(3)
    complete(0)
    multiply_out(3)
    add_near(0)
    add_relay(1)
    add_relay(2)
    add_twin(3)
    multiply_grads(0)
    turn(3)
    pass_on(2)
    add_near(1)
    add_near(2)
    add_relay(3)
    add_near(3)
    pass_on(3)
    multiply_grads(1)
    multiply_grads(2)
    for i in range(4):
        add_far(i)
    their_rows = pl.ds(pl.multiple_of(128 - me.core * 128, 128), 128)
    end = remote(final.at[their_rows], theirs, end_send, end_recv, twin)
    end.start()
    complete(1)
    complete(2)
    complete(3)
    multiply_grads(3)
    end.wait_recv()
    ours[...] = final[pl.ds(pl.multiple_of(me.core * 128, 128), 128)]

    @pl.when(me.core == 0)
    def _():
        block_out[:, :768] = ours[...]
        block_out[:, 768:] = theirs[...]

    @pl.when(me.core == 1)
    def _():
        block_out[:, :768] = theirs[...]
        block_out[:, 768:] = ours[...]

    @pl.when(is_home)
    def _():
        for t in range(4):
            gather(t, 0).wait_send()

    for t in range(4):
        for k in range(1, 5):
            gather(t, k).wait_send()
    for i in range(4):
        to_twin(i).wait_send()
        for d in (0, 1):
            rs1(i, d).wait_send()
            rs2(i, d).wait_send()
        rs3(i).wait_send()
    end.wait_send()


def combine(tokens, rows, w_out):
    dma = pltpu.SemaphoreType.DMA
    anywhere = pl.BlockSpec(memory_space=pl.ANY)
    vmem = pl.BlockSpec(memory_space=pltpu.VMEM)
    return pl.pallas_call(
        combine_kernel,
        name="combine",
        out_shape=(
            jax.ShapeDtypeStruct((128, 1536), BF16),
            jax.ShapeDtypeStruct((3, 1536, 384), F32),
            jax.ShapeDtypeStruct((3, 128, 1536), F32),
        ),
        in_specs=[anywhere, anywhere, vmem],
        out_specs=(vmem, vmem, vmem),
        scratch_shapes=[
            pltpu.VMEM((4, 3, 8, 256, 128), BF16),
            pltpu.VMEM((2, 8, 64, 1536), BF16),
            pltpu.VMEM((4, 1536, 512), BF16),
            pltpu.VMEM((4, 8, 64, 1536), BF16),
            pltpu.VMEM((384, 512), BF16),
            pltpu.VMEM((4, 2, 2, 4, 64, 768), BF16),
            pltpu.VMEM((4, 2, 4, 64, 768), BF16),
            pltpu.VMEM((4, 2, 64, 768), BF16),
            pltpu.VMEM((4, 2, 2, 64, 768), BF16),
            pltpu.VMEM((4, 64, 768), BF16),
            pltpu.VMEM((256, 768), BF16),
            pltpu.VMEM((128, 768), BF16),
            pltpu.VMEM((128, 768), BF16),
            dma((4,)), dma((4,)), dma((4,)),
            dma((4, 5)), dma((4, 5)),
            dma((4,)), dma((4,)),
            dma((4, 2)), dma((4, 2)),
            dma((4, 2)), dma((4, 2)),
            dma((4,)), dma((4,)),
            dma(()), dma(()),
        ],
        compiler_params=pltpu.CompilerParams(
            collective_id=3, has_side_effects=True, vmem_limit_bytes=62 << 20
        ),
    )(tokens.reshape(2, 8, 256, 1536), rows, w_out)


def local(inputs, w_qkv, w_out, grad_block):
    tokens, sums = project(inputs, grad_block, w_qkv, w_out)
    rows = attend_heads(sums)
    block_out, grad_qkv, grad_out = combine(tokens, rows, w_out)
    return block_out, jnp.transpose(grad_qkv, (1, 0, 2)), grad_out


def solution(mesh):
    placed = (P("row", "col"), P("col", "row", None), P("row", None, "col"), P("row", "col"))
    return jax.shard_map(
        local,
        mesh=mesh,
        in_specs=placed,
        out_specs=(P("row", "col"), P("col", "row", None), P("row", None, "col")),
        check_vma=False,
    )
```

time: 726 us -> 221 us (0.30)
  waiting for transfers between devices: 584 us -> 0 us
  Pallas kernels: 0 us -> 208 us
  matrix products: 93.3 us -> 0 us
  between operations: 14.3 us -> 0.66 us
  local copies, waits for them, and re-layouts: 21.3 us -> 9.75 us
  other arithmetic: 7.33 us -> 0 us
    reduce_scatter x5 -> x0, waiting for transfers between devices: 320 us -> none  [the longest x2 158 us: feature_sums(): lax.psum_scatter(term(jnp.int32(0), lax.axis_size('col') * rows_here).ast...]
    all_gather x5 -> x0, waiting for transfers between devices: 262 us -> none  [the longest x3 190 us: gather_heads(): return lax.all_gather(stacked, 'col', axis=1, tiled=True)]
    pallas_call x0 -> x3, Pallas kernels: none -> 208 us  [the longest x1 78.3 us: combine(): pl.pallas_call(combine_kernel, name='combine', out_shape=(jax.ShapeDtypeS...]
    dot_general x12 -> x0, matrix products: 86.7 us -> none  [the longest x1 14.2 us: backward_block(): jnp.einsum('hqk,qhd->khd', grad_scores, query_block, preferred_element_ty...]
    unnamed x12 -> x5, local copies, waits for them, and re-layouts: 15.6 us -> 9.75 us
  transfers between devices with their start and end apart: 10 -> 0, of which waited for: 10 -> 0; matrix products, arithmetic and copies ran while one was open for 15% -> 0% of each run, Pallas kernels for 0% -> 0%
where the time goes in v1:
time: 221 us; the launch traced here: 218 us
  Pallas kernels  208 us (94%)
  local copies, waits for them, and re-layouts  9.75 us (4%)
    pallas_call x1, Pallas kernels, combine(): pl.pallas_call(combine_kernel, name='combine', out_shape=(jax.ShapeDtypeS...  78.3 us
    pallas_call x1, Pallas kernels, project(): pl.pallas_call(project_kernel, name='project', out_shape=(jax.ShapeDtypeS...  77.7 us
    pallas_call x1, Pallas kernels, attend_heads(): pl.pallas_call(attend_kernel, name='attend', out_shape=jax.ShapeDtypeStru...  51.8 us
    unnamed x5, local copies, waits for them, and re-layouts  9.75 us

profile of v1, /device:TPU:17, one launch (start us, length us, event | category | flops | bytes accessed | tf_op | source)
XLA Modules:
  0.0 218.1 jit_solution(4988038680578654982)
XLA Ops:
  0.6 77.7 %project.1 = (bf16[2,16,128,1536]{3,2,1,0:T(8,128)(2,1)}, bf16[8,4,64,384]{3,2,1,0:T(8,128)(2,1)}) custom-call(bf16[128,1536]{1,0:T(8,128)(2,1)} %x_ref.1, bf16[128,1536]{1,0:T(8,128)(2,1)} %g_ref.1, bf16[3,1536,384]{2,1,0:T(8,128)(2,1)} %bitcast.5, bf16[3,128,1536]{2,1,0:T(8,128)(2,1)} %wo_ref.3), custom_call_target="tpu_custom_call" | custom-call | tf_op jit(solution)/shard_map/project/pallas_call | solution.py:303
  78.3 51.8 %attend.1.rows_hbm = bf16[4,3,8,64,128]{4,3,2,1,0:T(8,128)(2,1)} custom-call(bf16[8,4,64,384]{3,2,1,0:T(8,128)(2,1)} %get-tuple-element.9.rows_ref), custom_call_target="tpu_custom_call" | custom-call | tf_op jit(solution)/shard_map/attend/pallas_call | solution.py:552
  130.1 78.3 %combine.1 = (bf16[128,1536]{1,0:T(8,128)(2,1)}, f32[3,1536,384]{2,1,0:T(8,128)}, f32[3,128,1536]{2,1,0:T(8,128)}) custom-call(bf16[2,8,256,1536]{3,2,1,0:T(8,128)(2,1)} %bitcast.3, bf16[4,3,8,64,128]{4,3,2,1,0:T(8,128)(2,1)} %attend.1.rows_hbm, bf16[3,128,1536]{2,1,0:T(8,128)(2,1)} %wo_ref.3), custom_call_target="tpu_custom_call" | custom-call | tf_op jit(solution)/shard_map/combine/pallas_call | solution.py:827
  208.4 1.8 copy.10
  210.1 0.0 copy-start
  210.1 6.6 %copy.11 = f32[1536,3,384]{2,0,1:T(8,128)} copy(f32[1536,3,384]{2,0,1:T(8,128)} %bitcast.4) | data formatting | bytes 14155776
  216.7 0.0 copy-done
  216.7 1.4 copy.12
Async XLA Ops:
  210.1 6.6 %copy-start = (f32[3,128,1536]{2,1,0:T(8,128)S(1)}, f32[3,128,1536]{2,1,0:T(8,128)}, u32[]{:S(2)}) copy-start(f32[3,128,1536]{2,1,0:T(8,128)} %get-tuple-element.18) | copy-start | bytes 7077892

commit v2 on v0

v2 whole, which is shorter than its diff:
```python
import jax
import jax.numpy as jnp
from jax import lax
from jax.experimental import pallas as pl
from jax.experimental.pallas import tpu as pltpu
from jax.sharding import PartitionSpec as P

MESH = pl.DeviceIdType.MESH
BF16 = jnp.bfloat16
F32 = jnp.float32


class Place:
    def __init__(self):
        r = lax.axis_index("row")
        c = lax.axis_index("col")
        self.ylo, self.z, self.core = r // 8, (r // 2) % 4, r % 2
        self.yhi, self.x = c // 4, c % 4

    def at(self, ylo=0, z=0, core=0, yhi=0, x=0):
        return (
            lax.rem(self.ylo + ylo, 2) * 8 + lax.rem(self.z + z + 4, 4) * 2 + lax.rem(self.core + core, 2),
            lax.rem(self.yhi + yhi, 2) * 4 + lax.rem(self.x + x + 4, 4),
        )

    def slot(self, ylo=0, z=0, core=0):
        return self.at(ylo=ylo, z=z, core=core)[0]

    def col_x(self, x):
        return lax.rem(self.x + x + 4, 4)


def meet(partners):
    barrier = pltpu.get_barrier_semaphore()
    for partner in partners:
        pl.semaphore_signal(barrier, inc=1, device_id=partner, device_id_type=MESH)
    pl.semaphore_wait(barrier, len(partners))


def remote(src, dst, send, recv, device):
    return pltpu.make_async_remote_copy(
        src_ref=src, dst_ref=dst, send_sem=send, recv_sem=recv, device_id=device, device_id_type=MESH
    )


slice_at = (0, -1, 1, 2)


def block_kernel(
    x_ref, g_ref, w_hbm, wo_ref,
    x_out, grads_out, block_out, grad_out,
    held, part, relay, near, far, total, w_ref,
    kv, scores, slopes, grads, twin_grads, grads_relay, grads_near, result,
    wide, turned, block_relay, block_near, block_far, final, theirs,
    ag_send, ag_recv, s1_send, s1_recv, s2_send, s2_recv, s3_send, s3_recv, s4_send, s4_recv, x_sem, w_sem, own_sem,
    kv_send, kv_recv, tw_send, tw_recv, g1_send, g1_recv, g2_send, g2_recv, up_send, up_recv,
    wide_send, wide_recv, here_sem, out_sem, b0_send, b0_recv, b1_send, b1_recv, b2_send, b2_recv, b3_send, b3_recv,
    end_send, end_recv,
):
    me = Place()
    up, down, beside = me.at(z=1), me.at(z=-1), me.at(ylo=1)
    right, left, across, twin = me.at(x=1), me.at(x=-1), me.at(yhi=1), me.at(core=1)
    is_home = me.core == me.yhi
    is_away = jnp.logical_not(is_home)
    scale = 128 ** (-0.5)
    fill = -1e30
    own_rows = (x_ref, g_ref)
    low, high, every = pl.ds(0, 4), pl.ds(4, 4), pl.ds(0, 8)
    my_rows = pl.ds(pl.multiple_of(me.core * 32, 32), 32)
    their_rows = pl.ds(pl.multiple_of(32 - me.core * 32, 32), 32)

    def own(x=0):
        return pl.ds(pl.multiple_of(me.col_x(x) * 64, 64), 64)

    w_copy = pltpu.make_async_copy(w_hbm, w_ref, w_sem)
    w_copy.start()
    own_copy = []
    for a in (0, 1):
        copy = pltpu.make_async_copy(own_rows[a], held.at[a, pl.ds(me.slot() * 2, 2)], own_sem.at[a])
        copy.start()
        own_copy.append(copy)
    meet([beside, up, down, twin, right, left, across])

    def gather(a, k):
        slot, device = {
            0: (me.slot(), beside),
            1: (me.slot(), up),
            2: (me.slot(), down),
            3: (me.slot(ylo=1), up),
            4: (me.slot(ylo=1), down),
            5: (me.slot(z=-1), up),
            6: (me.slot(z=1), down),
            7: (me.slot(ylo=1, z=-1), up),
            8: (me.slot(ylo=1, z=1), down),
            9: (me.slot(), twin),
            10: (me.slot(ylo=1), twin),
            11: (me.slot(z=-1), twin),
            12: (me.slot(z=1), twin),
            13: (me.slot(ylo=1, z=-1), twin),
            14: (me.slot(ylo=1, z=1), twin),
            15: (me.slot(z=2), twin),
            16: (me.slot(ylo=1, z=2), twin),
        }[k]
        if k in (5, 7):
            rows = pl.ds(slot * 2, 1)
        elif k in (6, 8):
            rows = pl.ds(slot * 2 + 1, 1)
        else:
            rows = pl.ds(slot * 2, 2)
        ref = held.at[a, rows]
        src = own_rows[a] if k in (0, 1, 2, 9) else ref
        return remote(src, ref, ag_send.at[a, k], ag_recv.at[a, k], device)

    def go(a, *kinds):
        for k in kinds:
            gather(a, k).start()

    def landed(a, *kinds):
        for k in kinds:
            gather(a, k).wait_recv()

    def block_of(s):
        ylo = jnp.where((s == 1) | (s == 4) | (s == 5) | (s == 7), 1, 0)
        z = jnp.where((s == 2) | (s == 4), 3, jnp.where((s == 3) | (s == 5), 1, jnp.where(s >= 6, 2, 0)))
        return lax.rem(me.ylo + ylo, 2) * 4 + lax.rem(me.z + z, 4)

    def unit(a):
        return pl.ds(0, 3) if a == 0 else pl.ds(3, 1)

    def keep(s):
        block = pl.ds(block_of(s) * 4, 4)
        return pltpu.make_async_copy(held.at[0, block], x_out.at[block], x_sem.at[s])

    def rs1(a, s, d):
        rows = pl.ds(pl.multiple_of(me.col_x(2) * 64 + 32 * d, 32), 32)
        return remote(part.at[s, unit(a), rows], relay.at[s, d, unit(a)], s1_send.at[a, s, d], s1_recv.at[a, s, d], (right, left)[d])

    def rs2(a, s, d):
        return remote(part.at[s, unit(a), own((1, -1)[d])], near.at[s, d, unit(a)],
                      s2_send.at[a, s, d], s2_recv.at[a, s, d], (right, left)[d])

    def rs3(a, s):
        return remote(part.at[s, unit(a), own()], far.at[s, unit(a)], s3_send.at[a, s], s3_recv.at[a, s], across)

    def rs4(a, s):
        ref = total.at[block_of(s), unit(a)]
        return remote(ref, ref, s4_send.at[a, s], s4_recv.at[a, s], twin)

    def each(steps, body):
        lo, hi = steps
        if hi - lo == 1:
            body(lo)
        else:
            pl.loop(lo, hi)(body)

    def work(a, *steps):
        def body(s):
            remote(held.at[a, pl.ds(0, 2)], held.at[a, pl.ds(0, 2)], ag_send.at[a, 9 + s], ag_recv.at[a, 9 + s], twin).wait_recv()
            rows = held.at[a, pl.ds(block_of(s) * 4, 4)]
            if a == 0:
                keep(s).start()

                @pl.loop(0, 3)
                def _(h):
                    part[s, h] = jnp.dot(
                        rows[...].reshape(256, 1536), w_ref[h], preferred_element_type=F32
                    ).astype(BF16)
            else:
                part[s, 3] = lax.dot_general(
                    rows[...].reshape(256, 1536), wo_ref[...].reshape(384, 1536),
                    (((1,), (1,)), ((), ())), preferred_element_type=F32,
                ).astype(BF16)
            for d in (0, 1):
                rs1(a, s, d).start()
        each(steps, body)

    def add(ref, *terms):
        value = ref[...].astype(F32)
        for term in terms:
            value = value + term.astype(F32)
        ref[...] = value.astype(BF16)

    def add_relay(a, *steps):
        def body(s):
            for d in (0, 1):
                rs1(a, s, d).wait_recv()
                rows = pl.ds(pl.multiple_of(me.col_x((1, -1)[d]) * 64 + 32 * d, 32), 32)
                add(part.at[s, unit(a), rows], relay[s, d, unit(a)])
                rs2(a, s, d).start()
        each(steps, body)

    def add_near(a, *steps):
        def body(s):
            for d in (0, 1):
                rs2(a, s, d).wait_recv()
            add(part.at[s, unit(a), own()], near[s, 0, unit(a)], near[s, 1, unit(a)])

            @pl.when(is_away)
            def _():
                rs3(a, s).start()
        each(steps, body)

    def kv_gather(s, k):
        x, rows, device = {
            0: (0, 0, right),
            1: (0, 0, left),
            2: (-1, 1, right),
            3: (1, 2, left),
            4: (-1, 0, twin),
            5: (1, 0, twin),
            6: (2, 0, twin),
        }[k]
        start = me.col_x(x) * 64
        if rows == 0:
            span = pl.ds(pl.multiple_of(start, 64), 64)
        else:
            span = pl.ds(pl.multiple_of(start + 32 * (rows - 1), 32), 32)
        ref = kv.at[me.core, block_of(s), span]
        return remote(ref, ref, kv_send.at[s, k], kv_recv.at[s, k], device)

    def add_far(a, *steps):
        def body(s):
            block = block_of(s)

            @pl.when(is_home)
            def _():
                rs3(a, s).wait_recv()
                total[block, unit(a)] = (
                    part[s, unit(a), own()].astype(F32) + far[s, unit(a)].astype(F32)
                ).astype(BF16)
                rs4(a, s).start()

            @pl.when(is_away)
            def _():
                rs4(a, s).wait_recv()

            if a == 0:
                for j in (0, 1):
                    for h in range(3):
                        kv[j, block, own(), h * 128:(h + 1) * 128] = total[block, h, :, 128 + 128 * j:256 + 128 * j]
                kv_gather(s, 0).start()
                kv_gather(s, 1).start()
        each(steps, body)

    def kv_relay(*steps):
        def body(s):
            for d in (0, 1):
                kv_gather(s, d).wait_recv()
                kv_gather(s, 2 + d).start()
                kv_gather(s, 4 + d).start()
        each(steps, body)

    def kv_done(*steps):
        def body(s):
            kv_gather(s, 2).wait_recv()
            kv_gather(s, 3).wait_recv()
            kv_gather(s, 6).start()
        each(steps, body)

    def kv_whole(*steps):
        def body(s):
            for k in (4, 5, 6):
                kv_gather(s, k).wait_recv()
        each(steps, body)

    def attend(h):
        query = total[:, h, my_rows, 0:128].reshape(256, 128)
        cotangent = total[:, 3, my_rows, h * 128:(h + 1) * 128].reshape(256, 128)
        transposed = (((1,), (1,)), ((), ()))
        first = (((0,), (0,)), ((), ()))

        def masked(b, lanes):
            width = 256 - lanes
            s = lax.dot_general(kv[0, b, :, h * 128:(h + 1) * 128], query[lanes:], transposed, preferred_element_type=F32) * scale
            key_at = b * 256 + lax.broadcasted_iota(jnp.int32, (256, width), 0)
            column = lanes + lax.broadcasted_iota(jnp.int32, (1, width), 1)
            query_at = (column // 32) * 256 + me.x * 64 + me.core * 32 + column % 32
            return jnp.where(key_at <= query_at, s, fill)

        def top(lanes):
            def body(b, m):
                s = masked(b, lanes)
                scores[b, :, lanes:] = s
                return jnp.maximum(m, jnp.max(s, axis=0, keepdims=True))
            return body

        m = lax.fori_loop(0, 4, top(0), jnp.full((1, 256), fill, F32))
        m_high = lax.fori_loop(4, 8, top(128), m[:, 128:])
        m = jnp.concatenate([m[:, :128], m_high], axis=1)

        def sums(lanes, m):
            def body(b, carry):
                norm, slope = carry
                e = jnp.exp(scores[b, :, lanes:] - m)
                scores[b, :, lanes:] = e
                dp = lax.dot_general(kv[1, b, :, h * 128:(h + 1) * 128], cotangent[lanes:], transposed, preferred_element_type=F32)
                slopes[b, :, lanes:] = dp
                return (norm + jnp.sum(e, axis=0, keepdims=True), slope + jnp.sum(e * dp, axis=0, keepdims=True))
            return body

        zero = jnp.zeros((1, 256), F32)
        norm, slope = lax.fori_loop(0, 4, sums(0, m), (zero, zero))
        norm_high, slope_high = lax.fori_loop(4, 8, sums(128, m_high), (norm[:, 128:], slope[:, 128:]))
        norm = jnp.concatenate([norm[:, :128], norm_high], axis=1)
        slope = jnp.concatenate([slope[:, :128], slope_high], axis=1)
        inverse = 1.0 / norm
        slope = slope * inverse

        def backward(lanes):
            def body(b, carry):
                att, dq = carry
                p = scores[b, :, lanes:] * inverse[:, lanes:]
                w = p.astype(BF16)
                ds = (p * (slopes[b, :, lanes:] - slope[:, lanes:]) * scale).astype(BF16)
                grads[h, 0, b] = jnp.dot(ds, query[lanes:], preferred_element_type=F32).astype(BF16)
                grads[h, 1, b] = jnp.dot(w, cotangent[lanes:], preferred_element_type=F32).astype(BF16)
                att = att + lax.dot_general(kv[1, b, :, h * 128:(h + 1) * 128], w, first, preferred_element_type=F32)
                dq = dq + lax.dot_general(kv[0, b, :, h * 128:(h + 1) * 128], ds, first, preferred_element_type=F32)
                return att, dq
            return body

        square = jnp.zeros((128, 256), F32)
        att, dq = lax.fori_loop(0, 4, backward(0), (square, square))
        att_high, dq_high = lax.fori_loop(4, 8, backward(128), (att[:, 128:], dq[:, 128:]))
        for t, lo, hi in ((0, att, att_high), (1, dq, dq_high)):
            rows = jnp.concatenate([lo[:, :128], hi], axis=1).T.astype(BF16)
            result[t, h, :, my_rows] = rows.reshape(8, 32, 128)

    def to_twin(h):
        return remote(grads.at[h, 1 - me.core], twin_grads.at[h], tw_send.at[h], tw_recv.at[h], twin)

    def gs1(h, d):
        return remote(grads.at[h, me.core, (low, high)[d], own(2)], grads_relay.at[h, d],
                      g1_send.at[h, d], g1_recv.at[h, d], (right, left)[d])

    def gs2(h, d):
        return remote(grads.at[h, me.core, every, own((1, -1)[d])], grads_near.at[h, d],
                      g2_send.at[h, d], g2_recv.at[h, d], (right, left)[d])

    def add_twin(h):
        to_twin(h).wait_recv()

        @pl.loop(0, 8)
        def _(b):
            add(grads.at[h, me.core, b], twin_grads[h, b])

        for d in (0, 1):
            gs1(h, d).start()

    def add_grads_relay(h):
        for d in (0, 1):
            gs1(h, d).wait_recv()
            add(grads.at[h, me.core, (low, high)[d], own((1, -1)[d])], grads_relay[h, d])
            gs2(h, d).start()

    def add_grads_near(h):
        for d in (0, 1):
            gs2(h, d).wait_recv()
        result[2 + me.core, h] = (
            grads[h, me.core, :, own()].astype(F32) + grads_near[h, 0].astype(F32) + grads_near[h, 1].astype(F32)
        ).astype(BF16)

        @pl.when(is_away)
        def _():
            lift(h, 2).start()

    def lift(h, t):
        if t < 2:
            ref = result.at[t, h, every, my_rows]
        else:
            ref = result.at[2 + me.core, h]
        return remote(ref, ref, up_send.at[h, t], up_recv.at[h, t], twin)

    def lifted(h, t):
        ref = result.at[t, h, every, their_rows] if t < 2 else result.at[3 - me.core, h]
        remote(ref, ref, up_send.at[h, t], up_recv.at[h, t], twin).wait_recv()

    def after(h):
        to_twin(h).start()

        @pl.when(is_away)
        def _():
            lift(h, 0).start()
            lift(h, 1).start()

    def spread(h, t, k):
        x, blocks, device = {
            0: (0, every, across),
            1: (0, every, right),
            2: (0, every, left),
            3: (-1, low, right),
            4: (1, high, left),
        }[k]
        ref = wide.at[t, h, blocks, own(x)]
        src = result.at[t, h] if k == 0 else ref
        return remote(src, ref, wide_send.at[h, t, k], wide_recv.at[h, t, k], device)

    def here(h, t):
        return pltpu.make_async_copy(result.at[t, h], wide.at[t, h, every, own()], here_sem.at[h, t])

    def spread_home(h, types):
        @pl.when(is_home)
        def _():
            if types[0] < 2:
                lifted(h, 0)
                lifted(h, 1)
            else:
                lifted(h, 2)
            for t in types:
                spread(h, t, 0).start()
                here(h, t).start()
            for t in types:
                here(h, t).wait()
                spread(h, t, 1).start()
                spread(h, t, 2).start()

    def spread_away(h, types):
        @pl.when(is_away)
        def _():
            for t in types:
                spread(h, t, 0).wait_recv()
                spread(h, t, 1).start()
                spread(h, t, 2).start()

    def spread_relay(h, types):
        for t in types:
            for d in (0, 1):
                spread(h, t, 1 + d).wait_recv()
                spread(h, t, 3 + d).start()

    def keep_grads(h, t):
        return pltpu.make_async_copy(wide.at[t, h], grads_out.at[t - 1, h], out_sem.at[h, t - 1])

    def spread_done(h, types):
        for t in types:
            spread(h, t, 3).wait_recv()
            spread(h, t, 4).wait_recv()
            if t > 0:
                keep_grads(h, t).start()

    def block_lanes(core, n=None):
        if n is None:
            return pl.ds(pl.multiple_of(core * 768, 768), 768)
        return pl.ds(pl.multiple_of(core * 768 + n * 384, 384), 384)

    def b0(i, n):
        return remote(held.at[0, pl.ds(i * 8, 8), :, block_lanes(1 - me.core, n)], near.at[:, n, i],
                      b0_send.at[i, n], b0_recv.at[i, n], twin)

    def z_at(z):
        return lax.rem(me.z + z + 4, 4)

    def term_at(i, y, z):
        return held.at[0, i * 8 + y * 4 + z, :, block_lanes(me.core)]

    def b1(i, d):
        return remote(term_at(i, d, z_at(2)), block_relay.at[i, d], b1_send.at[i, d], b1_recv.at[i, d], (up, down)[d])

    def b2(i, d, y):
        return remote(term_at(i, y, z_at((1, -1)[d])), block_near.at[i, d, y], b2_send.at[i, d, y], b2_recv.at[i, d, y], (up, down)[d])

    def b3(i):
        return remote(term_at(i, 1 - me.ylo, me.z), block_far.at[i], b3_send.at[i], b3_recv.at[i], beside)

    def multiply_out(i):
        mine = jnp.concatenate([wide[0, h, :, own(slice_at[i])].reshape(512, 128) for h in range(3)], axis=1)
        turned[...] = mine.T

        @pl.loop(0, 4)
        def _(n):
            lanes = pl.ds(pl.multiple_of(n * 384, 384), 384)
            held[0, pl.ds(i * 8, 8), :, lanes] = jnp.dot(
                mine, wo_ref[:, :, lanes].reshape(384, 384), preferred_element_type=F32
            ).astype(BF16).reshape(8, 64, 384)

        b0(i, 0).start()
        b0(i, 1).start()

        @pl.loop(0, 4)
        def _(n):
            lanes = pl.ds(pl.multiple_of(n * 384, 384), 384)
            tokens = [held[1, b * 4 + me.col_x(slice_at[i]), :, lanes] for b in range(8)]
            term = jnp.dot(
                turned[...], jnp.concatenate(tokens, axis=0), preferred_element_type=F32
            ).reshape(3, 128, 384)
            if i == 0:
                grad_out[:, :, lanes] = term
            else:
                grad_out[:, :, lanes] += term

    def add_block_twin(i):
        for n in (0, 1):
            b0(i, n).wait_recv()

            @pl.loop(0, 8)
            def _(b):
                add(held.at[0, i * 8 + b, :, block_lanes(me.core, n)], near[b, n, i])

        for d in (0, 1):
            b1(i, d).start()

    def add_block_relay(i):
        for d in (0, 1):
            b2(i, d, 1 - d).start()
        for d in (0, 1):
            b1(i, d).wait_recv()
            add(term_at(i, d, z_at((1, -1)[d])), block_relay[i, d])
            b2(i, d, d).start()

    def add_block_near(i):
        for d in (0, 1):
            for y in (0, 1):
                b2(i, d, y).wait_recv()
        for y in (0, 1):
            add(term_at(i, y, me.z), block_near[i, 0, y], block_near[i, 1, y])
        b3(i).start()

    def add_block_far(i):
        b3(i).wait_recv()
        final[own(slice_at[i])] = (term_at(i, me.ylo, me.z)[...].astype(F32) + block_far[i].astype(F32)).astype(BF16)

    go(0, 9, 0, 1, 2)
    go(1, 9)
    w_copy.wait()
    for copy in own_copy:
        copy.wait()
    work(0, 0, 1)
    work(1, 0, 1)
    landed(0, 0)
    go(0, 3, 4, 10)
    go(1, 0)
    landed(0, 1)
    go(0, 5, 11)
    landed(0, 2)
    go(0, 6, 12)
    work(0, 1, 4)
    add_relay(0, 0, 1)
    add_relay(1, 0, 1)
    add_relay(0, 1, 3)
    landed(0, 3)
    go(0, 7, 13)
    landed(0, 4)
    go(0, 8, 14)
    go(1, 1, 2)
    work(0, 4, 6)
    add_relay(0, 3, 4)
    add_near(0, 0, 1)
    add_near(1, 0, 1)
    landed(0, 5, 6)
    go(0, 15)
    landed(1, 0)
    go(1, 3, 4, 10)
    landed(0, 7, 8)
    go(0, 16)
    work(0, 6, 8)
    work(1, 1, 2)
    add_near(0, 1, 4)
    add_relay(0, 4, 6)
    add_far(0, 0, 1)
    landed(1, 1)
    go(1, 5, 11)
    landed(1, 2)
    go(1, 6, 12)
    work(1, 2, 4)
    add_far(0, 1, 4)
    add_relay(0, 6, 8)
    add_near(0, 4, 6)
    kv_relay(0, 1)
    landed(1, 3)
    go(1, 7, 13)
    landed(1, 4)
    go(1, 8, 14)
    work(1, 4, 6)
    add_far(0, 4, 6)
    kv_relay(1, 4)
    add_near(0, 6, 8)
    add_relay(1, 1, 4)
    kv_done(0, 1)
    landed(1, 5, 6)
    go(1, 15)
    landed(1, 7, 8)
    go(1, 16)
    work(1, 6, 8)
    add_far(0, 6, 8)
    kv_relay(4, 6)
    kv_done(1, 4)
    add_relay(1, 4, 6)
    add_near(1, 1, 4)
    kv_relay(6, 8)
    kv_done(4, 6)
    add_relay(1, 6, 8)
    add_near(1, 4, 6)
    add_far(1, 0, 4)
    add_near(1, 6, 8)
    kv_done(6, 8)
    add_far(1, 4, 8)
    kv_whole(0, 8)

    first, second = (0, 1), (2, 3)
    attend(0)
    after(0)
    spread_home(0, first)
    add_twin(0)
    attend(1)
    after(1)
    spread_home(1, first)
    spread_away(0, first)
    add_twin(1)
    add_grads_relay(0)
    spread_relay(0, first)
    attend(2)
    after(2)
    spread_home(2, first)
    spread_away(1, first)
    add_twin(2)
    add_grads_relay(1)
    add_grads_near(0)
    spread_relay(1, first)
    spread_away(2, first)
    spread_home(0, second)
    for k in range(17):
        gather(0, k).wait_send()
    pl.loop(0, 8)(lambda s: keep(s).wait())
    multiply_out(0)
    spread_done(0, first)
    add_grads_relay(2)
    spread_relay(2, first)
    add_grads_near(1)
    spread_away(0, second)
    spread_home(1, second)
    add_block_twin(0)
    multiply_out(1)
    multiply_out(2)
    add_grads_near(2)
    spread_away(1, second)
    spread_home(2, second)
    spread_relay(0, second)
    add_block_twin(1)
    add_block_twin(2)
    add_block_relay(0)
    spread_away(2, second)
    spread_done(1, first)
    spread_done(2, first)
    multiply_out(3)
    spread_relay(1, second)
    add_block_near(0)
    add_block_relay(1)
    add_block_relay(2)
    add_block_twin(3)
    spread_relay(2, second)
    add_block_near(1)
    add_block_near(2)
    add_block_relay(3)
    for i in range(3):
        add_block_far(i)
    spread_done(0, second)
    spread_done(1, second)
    add_block_near(3)
    add_block_far(3)
    their_half = pl.ds(pl.multiple_of(128 - me.core * 128, 128), 128)
    end = remote(final.at[their_half], theirs, end_send, end_recv, twin)
    end.start()
    end.wait_recv()
    mine = final[pl.ds(pl.multiple_of(me.core * 128, 128), 128)]

    @pl.when(me.core == 0)
    def _():
        block_out[:, :768] = mine
        block_out[:, 768:] = theirs[...]

    @pl.when(me.core == 1)
    def _():
        block_out[:, :768] = theirs[...]
        block_out[:, 768:] = mine

    spread_done(2, second)

    @pl.when(is_away)
    def _():
        for a in (0, 1):
            pl.loop(0, 8)(lambda s: rs3(a, s).wait_send())
        for h in range(3):
            for t in range(3):
                lift(h, t).wait_send()

    @pl.when(is_home)
    def _():
        for a in (0, 1):
            pl.loop(0, 8)(lambda s: rs4(a, s).wait_send())
        for h in range(3):
            for t in range(4):
                spread(h, t, 0).wait_send()

    for k in range(17):
        gather(1, k).wait_send()

    @pl.loop(0, 8)
    def _(s):
        for a in (0, 1):
            for d in (0, 1):
                rs1(a, s, d).wait_send()
                rs2(a, s, d).wait_send()
        for k in range(7):
            kv_gather(s, k).wait_send()

    for h in range(3):
        to_twin(h).wait_send()
        for d in (0, 1):
            gs1(h, d).wait_send()
            gs2(h, d).wait_send()
        for t in range(4):
            for k in range(1, 5):
                spread(h, t, k).wait_send()
            if t > 0:
                keep_grads(h, t).wait()
    for i in range(4):
        for d in (0, 1):
            b0(i, d).wait_send()
            b1(i, d).wait_send()
            for y in (0, 1):
                b2(i, d, y).wait_send()
        b3(i).wait_send()
    end.wait_send()


def block(inputs, grad_block, w_qkv, w_out):
    dma = pltpu.SemaphoreType.DMA
    anywhere = pl.BlockSpec(memory_space=pl.ANY)
    vmem = pl.BlockSpec(memory_space=pltpu.VMEM)
    return pl.pallas_call(
        block_kernel,
        name="block",
        out_shape=(
            jax.ShapeDtypeStruct((32, 64, 1536), BF16),
            jax.ShapeDtypeStruct((3, 3, 8, 256, 128), BF16),
            jax.ShapeDtypeStruct((128, 1536), BF16),
            jax.ShapeDtypeStruct((3, 128, 1536), F32),
        ),
        in_specs=[vmem, vmem, anywhere, vmem],
        out_specs=(anywhere, anywhere, vmem, vmem),
        scratch_shapes=[
            pltpu.VMEM((2, 32, 64, 1536), BF16),
            pltpu.VMEM((8, 4, 256, 384), BF16),
            pltpu.VMEM((8, 2, 4, 32, 384), BF16),
            pltpu.VMEM((8, 2, 4, 64, 384), BF16),
            pltpu.VMEM((8, 4, 64, 384), BF16),
            pltpu.VMEM((8, 4, 64, 384), BF16),
            pltpu.VMEM((3, 1536, 384), BF16),
            pltpu.VMEM((2, 8, 256, 384), BF16),
            pltpu.VMEM((8, 256, 256), F32),
            pltpu.VMEM((8, 256, 256), F32),
            pltpu.VMEM((3, 2, 8, 256, 128), BF16),
            pltpu.VMEM((3, 8, 256, 128), BF16),
            pltpu.VMEM((3, 2, 4, 64, 128), BF16),
            pltpu.VMEM((3, 2, 8, 64, 128), BF16),
            pltpu.VMEM((4, 3, 8, 64, 128), BF16),
            pltpu.VMEM((4, 3, 8, 256, 128), BF16),
            pltpu.VMEM((384, 512), BF16),
            pltpu.VMEM((4, 2, 64, 768), BF16),
            pltpu.VMEM((4, 2, 2, 64, 768), BF16),
            pltpu.VMEM((4, 64, 768), BF16),
            pltpu.VMEM((256, 768), BF16),
            pltpu.VMEM((128, 768), BF16),
            dma((2, 17)), dma((2, 17)),
            dma((2, 8, 2)), dma((2, 8, 2)),
            dma((2, 8, 2)), dma((2, 8, 2)),
            dma((2, 8)), dma((2, 8)),
            dma((2, 8)), dma((2, 8)),
            dma((8,)), dma(()), dma((2,)),
            dma((8, 7)), dma((8, 7)),
            dma((3,)), dma((3,)),
            dma((3, 2)), dma((3, 2)),
            dma((3, 2)), dma((3, 2)),
            dma((3, 3)), dma((3, 3)),
            dma((3, 4, 5)), dma((3, 4, 5)),
            dma((3, 4)), dma((3, 3)),
            dma((4, 2)), dma((4, 2)),
            dma((4, 2)), dma((4, 2)),
            dma((4, 2, 2)), dma((4, 2, 2)),
            dma((4,)), dma((4,)),
            dma(()), dma(()),
        ],
        compiler_params=pltpu.CompilerParams(
            collective_id=1, has_side_effects=True, vmem_limit_bytes=63 << 20
        ),
    )(inputs.reshape(2, 64, 1536), grad_block.reshape(2, 64, 1536), jnp.transpose(w_qkv, (1, 0, 2)), w_out)


def weight_kernel(x_ref, rows_hbm, block_hbm, grad_out_hbm, out_ref, block_copy, grad_out_copy, rows, sem):
    step = pl.program_id(0)
    copies = [
        pltpu.make_async_copy(block_hbm, block_copy, sem.at[3]),
        pltpu.make_async_copy(grad_out_hbm, grad_out_copy, sem.at[4]),
    ]

    @pl.when(step == 0)
    def _():
        loads = [pltpu.make_async_copy(rows_hbm.at[:, h], rows.at[h], sem.at[h]) for h in range(3)]
        for load in loads:
            load.start()
        for copy in copies:
            copy.start()
        for load in loads:
            load.wait()

    turned = x_ref[...].reshape(2048, 256).T
    for h in range(3):
        factor = jnp.concatenate([rows[h, t].reshape(2048, 128) for t in range(3)], axis=1)
        out_ref[h] = jnp.dot(turned, factor, preferred_element_type=F32)

    @pl.when(step == pl.num_programs(0) - 1)
    def _():
        for copy in copies:
            copy.wait()


def weight_grad(tokens, rows, block_rows, grad_out):
    anywhere = pl.BlockSpec(memory_space=pl.ANY)
    return pl.pallas_call(
        weight_kernel,
        name="weight_grad",
        grid=(6,),
        out_shape=(
            jax.ShapeDtypeStruct((3, 1536, 384), F32),
            jax.ShapeDtypeStruct((128, 1536), BF16),
            jax.ShapeDtypeStruct((3, 128, 1536), F32),
        ),
        in_specs=[pl.BlockSpec((32, 64, 256), lambda m: (0, 0, m)), anywhere, anywhere, anywhere],
        out_specs=(pl.BlockSpec((3, 256, 384), lambda m: (0, m, 0)), anywhere, anywhere),
        scratch_shapes=[pltpu.VMEM((3, 3, 8, 256, 128), BF16), pltpu.SemaphoreType.DMA((5,))],
        compiler_params=pltpu.CompilerParams(vmem_limit_bytes=48 << 20),
    )(tokens, rows, block_rows, grad_out)


def local(inputs, w_qkv, w_out, grad_block):
    tokens, rows, block_rows, grad_out = block(inputs, grad_block, w_qkv, w_out)
    grad_qkv, block_out, grad_out = weight_grad(tokens, rows, block_rows, grad_out)
    return block_out, jnp.transpose(grad_qkv, (1, 0, 2)), grad_out


def solution(mesh):
    placed = (P("row", "col"), P("col", "row", None), P("row", None, "col"), P("row", "col"))
    return jax.shard_map(
        local,
        mesh=mesh,
        in_specs=placed,
        out_specs=(P("row", "col"), P("col", "row", None), P("row", None, "col")),
        check_vma=False,
    )
```

time: 726 us -> 206 us (0.28)
  waiting for transfers between devices: 584 us -> 0 us
  Pallas kernels: 0 us -> 202 us
  matrix products: 93.3 us -> 0 us
  local copies, waits for them, and re-layouts: 21.3 us -> 2.65 us
  between operations: 14.3 us -> 0.81 us
  other arithmetic: 7.33 us -> 0 us
    reduce_scatter x5 -> x0, waiting for transfers between devices: 320 us -> none  [the longest x2 158 us: feature_sums(): lax.psum_scatter(term(jnp.int32(0), lax.axis_size('col') * rows_here).ast...]
    all_gather x5 -> x0, waiting for transfers between devices: 262 us -> none  [the longest x3 190 us: gather_heads(): return lax.all_gather(stacked, 'col', axis=1, tiled=True)]
    pallas_call x0 -> x2, Pallas kernels: none -> 202 us  [the longest x1 185 us: block(): pl.pallas_call(block_kernel, name='block', out_shape=(jax.ShapeDtypeStruc...]
    dot_general x12 -> x0, matrix products: 86.7 us -> none  [the longest x1 14.2 us: backward_block(): jnp.einsum('hqk,qhd->khd', grad_scores, query_block, preferred_element_ty...]
    unnamed x12 -> x4, local copies, waits for them, and re-layouts: 15.6 us -> 2.65 us
  transfers between devices with their start and end apart: 10 -> 0, of which waited for: 10 -> 0; matrix products, arithmetic and copies ran while one was open for 15% -> 0% of each run, Pallas kernels for 0% -> 0%
where the time goes in v2:
time: 206 us
  Pallas kernels  202 us (98%)
  local copies, waits for them, and re-layouts  2.65 us (1%)
    pallas_call x1, Pallas kernels, block(): pl.pallas_call(block_kernel, name='block', out_shape=(jax.ShapeDtypeStruc...  185 us
    pallas_call x1, Pallas kernels, weight_grad(): pl.pallas_call(weight_kernel, name='weight_grad', grid=(6,), out_shape=(j...  16.9 us

profile of v2, /device:TPU:17, one launch (start us, length us, event | category | flops | bytes accessed | tf_op | source)
XLA Modules:
  0.0 205.8 jit_solution(10414214007057519769)
XLA Ops:
  0.6 185.4 %block.1 = (bf16[32,64,1536]{2,1,0:T(8,128)(2,1)}, bf16[3,3,8,256,128]{4,3,2,1,0:T(8,128)(2,1)}, bf16[128,1536]{1,0:T(8,128)(2,1)}, f32[3,128,1536]{2,1,0:T(8,128)}) custom-call(bf16[2,64,1536]{2,1,0:T(8,128)(2,1)} %bitcast.5, bf16[2,64,1536]{2,1,0:T(8,128)(2,1)} %bitcast.6, bf16[3,1536,384]{2,1,0:T(8,128)(2,1)} %bitcast.4, bf16[3,128,1536]{2,1,0:T(8,128)(2,1)} %wo_ref.1), custom_call_target="tpu_custom_call" | custom-call | tf_op jit(solution)/shard_map/block/pallas_call | solution.py:730
  186.0 0.0 copy-start
  186.0 1.7 copy-done
  187.7 0.0 copy-start.1
  187.7 1.0 copy-done.1
  188.7 16.9 %weight_grad.1 = (f32[3,1536,384]{2,1,0:T(8,128)}, bf16[128,1536]{1,0:T(8,128)(2,1)}, f32[3,128,1536]{2,1,0:T(8,128)}) custom-call(bf16[32,64,1536]{2,1,0:T(8,128)(2,1)} %get-tuple-element.10.x_ref, bf16[3,3,8,256,128]{4,3,2,1,0:T(8,128)(2,1)} %get-tuple-element.11.rows_hbm, bf16[128,1536]{1,0:T(8,128)(2,1)S(1)} %copy-done.1, f32[3,128,1536]{2,1,0:T(8,128)S(1)} %copy-done), custom_call_target="tpu_custom_call" | custom-call | tf_op jit(solution)/shard_map/weight_grad/pallas_call | solution.py:819
Async XLA Ops:
  186.0 1.7 copy-start
  187.7 1.0 copy-start.1

commit v3 on v2

--- a/solution.py
+++ b/solution.py
@@ -44,15 +44,17 @@
 
 
 slice_at = (0, -1, 1, 2)
+along_x_first = (1,)
+across_first = ()
 
 
 def block_kernel(
-    x_ref, g_ref, w_hbm, wo_ref,
-    x_out, grads_out, block_out, grad_out,
-    held, part, relay, near, far, total, w_ref,
+    x_hbm, g_hbm, w_hbm, wo_hbm,
+    turned_out, grads_out, block_hbm, grad_out_hbm,
+    held, part, relay, near, far, crossed, total, w_ref, wo_ref, block_out, grad_out,
     kv, scores, slopes, grads, twin_grads, grads_relay, grads_near, result,
     wide, turned, block_relay, block_near, block_far, final, theirs,
-    ag_send, ag_recv, s1_send, s1_recv, s2_send, s2_recv, s3_send, s3_recv, s4_send, s4_recv, x_sem, w_sem, own_sem,
+    ag_send, ag_recv, s1_send, s1_recv, s2_send, s2_recv, s3_send, s3_recv, s4_send, s4_recv, x_sem, w_sem, own_sem, cross_send, cross_recv, last_sem,
     kv_send, kv_recv, tw_send, tw_recv, g1_send, g1_recv, g2_send, g2_recv, up_send, up_recv,
     wide_send, wide_recv, here_sem, out_sem, b0_send, b0_recv, b1_send, b1_recv, b2_send, b2_recv, b3_send, b3_recv,
     end_send, end_recv,
@@ -64,7 +66,6 @@
     is_away = jnp.logical_not(is_home)
     scale = 128 ** (-0.5)
     fill = -1e30
-    own_rows = (x_ref, g_ref)
     low, high, every = pl.ds(0, 4), pl.ds(4, 4), pl.ds(0, 8)
     my_rows = pl.ds(pl.multiple_of(me.core * 32, 32), 32)
     their_rows = pl.ds(pl.multiple_of(32 - me.core * 32, 32), 32)
@@ -72,13 +73,16 @@
     def own(x=0):
         return pl.ds(pl.multiple_of(me.col_x(x) * 64, 64), 64)
 
-    w_copy = pltpu.make_async_copy(w_hbm, w_ref, w_sem)
+    own_copy = [
+        pltpu.make_async_copy(ref, held.at[a, pl.ds(me.slot() * 2, 2)], own_sem.at[a])
+        for a, ref in enumerate((x_hbm, g_hbm))
+    ]
+    w_copy = pltpu.make_async_copy(w_hbm, w_ref, w_sem.at[0])
+    wo_copy = pltpu.make_async_copy(wo_hbm, wo_ref, w_sem.at[1])
+    own_copy[0].start()
     w_copy.start()
-    own_copy = []
-    for a in (0, 1):
-        copy = pltpu.make_async_copy(own_rows[a], held.at[a, pl.ds(me.slot() * 2, 2)], own_sem.at[a])
-        copy.start()
-        own_copy.append(copy)
+    own_copy[1].start()
+    wo_copy.start()
     meet([beside, up, down, twin, right, left, across])
 
     def gather(a, k):
@@ -108,8 +112,7 @@
         else:
             rows = pl.ds(slot * 2, 2)
         ref = held.at[a, rows]
-        src = own_rows[a] if k in (0, 1, 2, 9) else ref
-        return remote(src, ref, ag_send.at[a, k], ag_recv.at[a, k], device)
+        return remote(ref, ref, ag_send.at[a, k], ag_recv.at[a, k], device)
 
     def go(a, *kinds):
         for k in kinds:
@@ -128,8 +131,21 @@
         return pl.ds(0, 3) if a == 0 else pl.ds(3, 1)
 
     def keep(s):
-        block = pl.ds(block_of(s) * 4, 4)
-        return pltpu.make_async_copy(held.at[0, block], x_out.at[block], x_sem.at[s])
+        columns = pl.ds(pl.multiple_of(block_of(s) * 256, 256), 256)
+        return pltpu.make_async_copy(w_ref.at[s % 3, :, 0:256], turned_out.at[:, columns], x_sem.at[s])
+
+    def turn(*steps):
+        for s in range(*steps):
+            if s >= 3:
+                keep(s - 3).wait()
+
+            @pl.loop(0, 12)
+            def _(n):
+                lanes = pl.ds(pl.multiple_of(n * 128, 128), 128)
+                rows = held[0, pl.ds(block_of(s) * 4, 4), :, lanes].reshape(256, 128)
+                w_ref[s % 3, lanes, 0:256] = rows.T
+
+            keep(s).start()
 
     def rs1(a, s, d):
         rows = pl.ds(pl.multiple_of(me.col_x(2) * 64 + 32 * d, 32), 32)
@@ -145,6 +161,13 @@
     def rs4(a, s):
         ref = total.at[block_of(s), unit(a)]
         return remote(ref, ref, s4_send.at[a, s], s4_recv.at[a, s], twin)
+
+    def is_crossed(a, steps):
+        return a == 0 and steps[0] in across_first
+
+    def cross(s):
+        return remote(part.at[s, unit(0)], crossed.at[s - min(across_first)],
+                      cross_send.at[s - min(across_first)], cross_recv.at[s - min(across_first)], across)
 
     def each(steps, body):
         lo, hi = steps
@@ -158,8 +181,6 @@
             remote(held.at[a, pl.ds(0, 2)], held.at[a, pl.ds(0, 2)], ag_send.at[a, 9 + s], ag_recv.at[a, 9 + s], twin).wait_recv()
             rows = held.at[a, pl.ds(block_of(s) * 4, 4)]
             if a == 0:
-                keep(s).start()
-
                 @pl.loop(0, 3)
                 def _(h):
                     part[s, h] = jnp.dot(
@@ -170,9 +191,23 @@
                     rows[...].reshape(256, 1536), wo_ref[...].reshape(384, 1536),
                     (((1,), (1,)), ((), ())), preferred_element_type=F32,
                 ).astype(BF16)
-            for d in (0, 1):
-                rs1(a, s, d).start()
+            if is_crossed(a, steps):
+                pl.when(is_away)(lambda: cross(s).start())
+            else:
+                for d in (0, 1):
+                    rs1(a, s, d).start()
         each(steps, body)
+
+    def add_crossed(*steps):
+        @pl.when(is_home)
+        def _():
+            def body(s):
+                cross(s).wait_recv()
+                for h in range(3):
+                    add(part.at[s, h], crossed[s - min(across_first), h])
+                for d in (0, 1):
+                    rs1(0, s, d).start()
+            each(steps, body)
 
     def add(ref, *terms):
         value = ref[...].astype(F32)
@@ -187,18 +222,22 @@
                 rows = pl.ds(pl.multiple_of(me.col_x((1, -1)[d]) * 64 + 32 * d, 32), 32)
                 add(part.at[s, unit(a), rows], relay[s, d, unit(a)])
                 rs2(a, s, d).start()
-        each(steps, body)
+        if is_crossed(a, steps):
+            pl.when(is_home)(lambda: each(steps, body))
+        else:
+            each(steps, body)
 
     def add_near(a, *steps):
         def body(s):
             for d in (0, 1):
                 rs2(a, s, d).wait_recv()
             add(part.at[s, unit(a), own()], near[s, 0, unit(a)], near[s, 1, unit(a)])
-
-            @pl.when(is_away)
-            def _():
-                rs3(a, s).start()
-        each(steps, body)
+            if not is_crossed(a, steps):
+                pl.when(is_away)(lambda: rs3(a, s).start())
+        if is_crossed(a, steps):
+            pl.when(is_home)(lambda: each(steps, body))
+        else:
+            each(steps, body)
 
     def kv_gather(s, k):
         x, rows, device = {
@@ -224,10 +263,13 @@
 
             @pl.when(is_home)
             def _():
-                rs3(a, s).wait_recv()
-                total[block, unit(a)] = (
-                    part[s, unit(a), own()].astype(F32) + far[s, unit(a)].astype(F32)
-                ).astype(BF16)
+                if is_crossed(a, steps):
+                    total[block, unit(a)] = part[s, unit(a), own()]
+                else:
+                    rs3(a, s).wait_recv()
+                    total[block, unit(a)] = (
+                        part[s, unit(a), own()].astype(F32) + far[s, unit(a)].astype(F32)
+                    ).astype(BF16)
                 rs4(a, s).start()
 
             @pl.when(is_away)
@@ -390,6 +432,9 @@
             2: (0, every, left),
             3: (-1, low, right),
             4: (1, high, left),
+            5: (-1, every, across),
+            6: (1, every, across),
+            7: (2, every, across),
         }[k]
         ref = wide.at[t, h, blocks, own(x)]
         src = result.at[t, h] if k == 0 else ref
@@ -401,12 +446,9 @@
     def spread_home(h, types):
         @pl.when(is_home)
         def _():
-            if types[0] < 2:
-                lifted(h, 0)
-                lifted(h, 1)
-            else:
-                lifted(h, 2)
             for t in types:
+                if t < 3:
+                    lifted(h, t)
                 spread(h, t, 0).start()
                 here(h, t).start()
             for t in types:
@@ -419,22 +461,62 @@
         def _():
             for t in types:
                 spread(h, t, 0).wait_recv()
-                spread(h, t, 1).start()
-                spread(h, t, 2).start()
+                if t not in along_x_first:
+                    spread(h, t, 1).start()
+                    spread(h, t, 2).start()
 
     def spread_relay(h, types):
-        for t in types:
+        def around(t):
             for d in (0, 1):
                 spread(h, t, 1 + d).wait_recv()
                 spread(h, t, 3 + d).start()
+                if t in along_x_first:
+                    spread(h, t, 5 + d).start()
+
+        for t in types:
+            if t not in along_x_first:
+                around(t)
+
+        def home_rows():
+            for t in types:
+                if t in along_x_first:
+                    around(t)
+
+        def away_rows():
+            for t in types:
+                if t in along_x_first:
+                    spread(h, t, 5).wait_recv()
+                    spread(h, t, 6).wait_recv()
+
+        pl.when(is_home)(home_rows)
+        pl.when(is_away)(away_rows)
 
     def keep_grads(h, t):
-        return pltpu.make_async_copy(wide.at[t, h], grads_out.at[t - 1, h], out_sem.at[h, t - 1])
+        lanes = pl.ds(h * 384 + (t - 1) * 128, 128)
+        return pltpu.make_async_copy(wide.at[t, h], grads_out.at[:, :, lanes], out_sem.at[h, t - 1])
 
     def spread_done(h, types):
-        for t in types:
+        def arrived(t):
             spread(h, t, 3).wait_recv()
             spread(h, t, 4).wait_recv()
+
+        def home_rows():
+            for t in types:
+                if t in along_x_first:
+                    arrived(t)
+                    spread(h, t, 7).start()
+
+        def away_rows():
+            for t in types:
+                if t in along_x_first:
+                    spread(h, t, 7).wait_recv()
+
+        for t in types:
+            if t not in along_x_first:
+                arrived(t)
+        pl.when(is_home)(home_rows)
+        pl.when(is_away)(away_rows)
+        for t in types:
             if t > 0:
                 keep_grads(h, t).start()
 
@@ -519,143 +601,218 @@
         b3(i).wait_recv()
         final[own(slice_at[i])] = (term_at(i, me.ylo, me.z)[...].astype(F32) + block_far[i].astype(F32)).astype(BF16)
 
+    own_copy[0].wait()
     go(0, 9, 0, 1, 2)
+    w_copy.wait()
+    work(0, 0, 1)
+    own_copy[1].wait()
     go(1, 9)
-    w_copy.wait()
-    for copy in own_copy:
-        copy.wait()
-    work(0, 0, 1)
+    wo_copy.wait()
     work(1, 0, 1)
+    add_relay(0, 0, 1)
     landed(0, 0)
     go(0, 3, 4, 10)
-    go(1, 0)
+    add_relay(1, 0, 1)
+    landed(0, 2)
+    go(0, 6, 12)
+    work(0, 1, 2)
     landed(0, 1)
     go(0, 5, 11)
-    landed(0, 2)
-    go(0, 6, 12)
-    work(0, 1, 4)
-    add_relay(0, 0, 1)
-    add_relay(1, 0, 1)
-    add_relay(0, 1, 3)
+    add_near(0, 0, 1)
+    work(0, 2, 4)
+    add_relay(0, 1, 2)
+    add_relay(0, 3, 4)
+    go(1, 1, 2)
     landed(0, 3)
     go(0, 7, 13)
+    add_relay(0, 2, 3)
+    landed(0, 5, 6)
+    go(0, 15)
     landed(0, 4)
     go(0, 8, 14)
-    go(1, 1, 2)
+    go(1, 0)
     work(0, 4, 6)
-    add_relay(0, 3, 4)
-    add_near(0, 0, 1)
-    add_near(1, 0, 1)
-    landed(0, 5, 6)
-    go(0, 15)
+    add_near(0, 3, 4)
+    add_far(0, 0, 1)
+    work(0, 6, 7)
+    add_near(0, 1, 2)
+    add_relay(0, 4, 5)
+    kv_relay(0, 1)
+    landed(0, 7, 8)
+    go(0, 16)
+    add_near(0, 2, 3)
     landed(1, 0)
     go(1, 3, 4, 10)
-    landed(0, 7, 8)
-    go(0, 16)
-    work(0, 6, 8)
-    work(1, 1, 2)
-    add_near(0, 1, 4)
-    add_relay(0, 4, 6)
-    add_far(0, 0, 1)
+    landed(1, 2)
+    go(1, 6, 12)
     landed(1, 1)
     go(1, 5, 11)
-    landed(1, 2)
-    go(1, 6, 12)
-    work(1, 2, 4)
-    add_far(0, 1, 4)
-    add_relay(0, 6, 8)
-    add_near(0, 4, 6)
-    kv_relay(0, 1)
+    add_far(0, 3, 4)
+    add_far(0, 1, 2)
+    add_near(1, 0, 1)
+    add_relay(0, 5, 6)
+    add_near(0, 4, 5)
+    work(1, 1, 2)
+    work(0, 7, 8)
+    add_relay(0, 6, 7)
+    work(1, 3, 4)
+    landed(1, 4)
+    go(1, 8, 14)
     landed(1, 3)
     go(1, 7, 13)
-    landed(1, 4)
-    go(1, 8, 14)
-    work(1, 4, 6)
-    add_far(0, 4, 6)
-    kv_relay(1, 4)
-    add_near(0, 6, 8)
-    add_relay(1, 1, 4)
-    kv_done(0, 1)
+    add_relay(0, 7, 8)
+    add_far(0, 2, 3)
+    add_far(0, 4, 5)
+    add_near(0, 5, 6)
+    kv_relay(2, 3)
     landed(1, 5, 6)
     go(1, 15)
+    add_relay(1, 1, 2)
+    kv_relay(3, 4)
+    kv_relay(1, 2)
+    work(1, 2, 3)
+    work(1, 5, 6)
+    add_near(0, 7, 8)
+    add_far(0, 5, 6)
+    add_relay(1, 2, 3)
+    kv_done(1, 2)
+    add_near(0, 6, 7)
+    work(1, 4, 5)
+    kv_relay(4, 5)
     landed(1, 7, 8)
     go(1, 16)
-    work(1, 6, 8)
-    add_far(0, 6, 8)
-    kv_relay(4, 6)
-    kv_done(1, 4)
-    add_relay(1, 4, 6)
-    add_near(1, 1, 4)
+    add_near(1, 1, 2)
+    kv_relay(5, 6)
+    kv_done(2, 3)
+    add_relay(1, 3, 4)
+    add_relay(1, 5, 6)
+    kv_done(4, 5)
+    kv_done(3, 4)
+    work(1, 6, 7)
+    kv_done(5, 6)
+    add_far(0, 7, 8)
+    add_far(1, 0, 1)
+    kv_whole(4, 5)
+    add_relay(1, 4, 5)
+    add_near(1, 3, 4)
+    work(1, 7, 8)
+    kv_done(0, 1)
+    add_near(1, 5, 6)
+    add_relay(1, 6, 7)
+    add_near(1, 2, 3)
+    add_far(0, 6, 7)
+    turn(0, 1)
+    add_far(1, 1, 2)
+    turn(1, 2)
+    add_relay(1, 7, 8)
+    kv_whole(0, 1)
+    add_near(1, 4, 5)
+    add_near(1, 6, 7)
     kv_relay(6, 8)
-    kv_done(4, 6)
-    add_relay(1, 6, 8)
-    add_near(1, 4, 6)
-    add_far(1, 0, 4)
-    add_near(1, 6, 8)
-    kv_done(6, 8)
-    add_far(1, 4, 8)
-    kv_whole(0, 8)
-
-    first, second = (0, 1), (2, 3)
+    kv_whole(2, 3)
+    add_near(1, 7, 8)
+    add_far(1, 3, 4)
+    kv_done(6, 7)
+    add_far(1, 2, 3)
+    kv_whole(1, 2)
+    add_far(1, 5, 6)
+    kv_done(7, 8)
+    add_far(1, 6, 7)
+    add_far(1, 4, 5)
+    add_far(1, 7, 8)
+    kv_whole(3, 4)
+    kv_whole(6, 8)
+    kv_whole(5, 6)
     attend(0)
     after(0)
-    spread_home(0, first)
+    spread_home(0, (0,))
+    spread_home(0, (1,))
     add_twin(0)
     attend(1)
+    add_grads_relay(0)
     after(1)
-    spread_home(1, first)
-    spread_away(0, first)
-    add_twin(1)
-    add_grads_relay(0)
-    spread_relay(0, first)
+    spread_home(1, (0,))
+    spread_home(1, (1,))
+    spread_away(0, (1,))
     attend(2)
     after(2)
-    spread_home(2, first)
-    spread_away(1, first)
+    spread_home(2, (0,))
+    add_twin(1)
+    spread_away(0, (0,))
+    spread_away(1, (1,))
+    spread_away(1, (0,))
+    add_grads_near(0)
+    spread_relay(1, (0,))
+    turn(2, 3)
+    spread_home(2, (1,))
+    turn(3, 4)
+    turn(4, 5)
+    spread_away(2, (0,))
+    spread_relay(0, (1,))
+    turn(5, 6)
+    turn(6, 7)
+    turn(7, 8)
     add_twin(2)
+    spread_relay(1, (1,))
     add_grads_relay(1)
-    add_grads_near(0)
-    spread_relay(1, first)
-    spread_away(2, first)
-    spread_home(0, second)
+    spread_away(2, (1,))
     for k in range(17):
         gather(0, k).wait_send()
-    pl.loop(0, 8)(lambda s: keep(s).wait())
     multiply_out(0)
-    spread_done(0, first)
+    spread_relay(2, (1,))
+    add_grads_near(1)
+    spread_home(0, (2,))
+    spread_relay(2, (0,))
+    spread_relay(0, (0,))
+    add_block_twin(0)
     add_grads_relay(2)
-    spread_relay(2, first)
-    add_grads_near(1)
-    spread_away(0, second)
-    spread_home(1, second)
-    add_block_twin(0)
     multiply_out(1)
+    add_block_relay(0)
+    spread_home(1, (2,))
+    spread_home(1, (3,))
     multiply_out(2)
+    spread_done(1, (0,))
+    spread_home(0, (3,))
+    add_block_twin(1)
     add_grads_near(2)
-    spread_away(1, second)
-    spread_home(2, second)
-    spread_relay(0, second)
-    add_block_twin(1)
+    spread_home(2, (2,))
+    spread_home(2, (3,))
+    spread_done(0, (0,))
+    spread_away(0, (2,))
     add_block_twin(2)
-    add_block_relay(0)
-    spread_away(2, second)
-    spread_done(1, first)
-    spread_done(2, first)
+    spread_away(1, (2,))
+    spread_done(2, (0,))
+    spread_away(0, (3,))
+    add_block_near(0)
+    spread_away(1, (3,))
+    spread_done(1, (1,))
+    spread_away(2, (2,))
+    add_block_relay(1)
+    spread_away(2, (3,))
+    add_block_relay(2)
     multiply_out(3)
-    spread_relay(1, second)
-    add_block_near(0)
-    add_block_relay(1)
-    add_block_relay(2)
+    grad_out_copy = pltpu.make_async_copy(grad_out, grad_out_hbm, last_sem.at[0])
+    grad_out_copy.start()
+    spread_done(2, (1,))
+    spread_relay(0, (3,))
     add_block_twin(3)
-    spread_relay(2, second)
     add_block_near(1)
+    spread_relay(2, (3,))
+    spread_relay(1, (2,))
     add_block_near(2)
+    spread_relay(0, (2,))
     add_block_relay(3)
-    for i in range(3):
-        add_block_far(i)
-    spread_done(0, second)
-    spread_done(1, second)
+    spread_done(0, (1,))
+    spread_relay(1, (3,))
     add_block_near(3)
+    spread_done(2, (3,))
+    add_block_far(2)
+    spread_relay(2, (2,))
+    spread_done(1, (2,))
+    add_block_far(0)
+    spread_done(2, (2,))
+    spread_done(0, (2,))
+    add_block_far(1)
     add_block_far(3)
     their_half = pl.ds(pl.multiple_of(128 - me.core * 128, 128), 128)
     end = remote(final.at[their_half], theirs, end_send, end_recv, twin)
@@ -673,12 +830,25 @@
         block_out[:, :768] = theirs[...]
         block_out[:, 768:] = mine
 
-    spread_done(2, second)
+    block_copy = pltpu.make_async_copy(block_out, block_hbm, last_sem.at[1])
+    block_copy.start()
+    spread_done(0, (3,))
+    spread_done(1, (3,))
+
+    def sums_sent(a, s):
+        for d in (0, 1):
+            rs1(a, s, d).wait_send()
+            rs2(a, s, d).wait_send()
 
     @pl.when(is_away)
     def _():
-        for a in (0, 1):
-            pl.loop(0, 8)(lambda s: rs3(a, s).wait_send())
+        for s in range(8):
+            for a in (0, 1):
+                if a == 0 and s in across_first:
+                    cross(s).wait_send()
+                else:
+                    rs3(a, s).wait_send()
+                    sums_sent(a, s)
         for h in range(3):
             for t in range(3):
                 lift(h, t).wait_send()
@@ -686,20 +856,22 @@
     @pl.when(is_home)
     def _():
         for a in (0, 1):
-            pl.loop(0, 8)(lambda s: rs4(a, s).wait_send())
+            @pl.loop(0, 8)
+            def _(s):
+                rs4(a, s).wait_send()
+                sums_sent(a, s)
         for h in range(3):
             for t in range(4):
                 spread(h, t, 0).wait_send()
+                if t in along_x_first:
+                    for k in range(1, 8):
+                        spread(h, t, k).wait_send()
 
     for k in range(17):
         gather(1, k).wait_send()
 
     @pl.loop(0, 8)
     def _(s):
-        for a in (0, 1):
-            for d in (0, 1):
-                rs1(a, s, d).wait_send()
-                rs2(a, s, d).wait_send()
         for k in range(7):
             kv_gather(s, k).wait_send()
 
@@ -709,8 +881,9 @@
             gs1(h, d).wait_send()
             gs2(h, d).wait_send()
         for t in range(4):
-            for k in range(1, 5):
-                spread(h, t, k).wait_send()
+            if t not in along_x_first:
+                for k in range(1, 5):
+                    spread(h, t, k).wait_send()
             if t > 0:
                 keep_grads(h, t).wait()
     for i in range(4):
@@ -720,32 +893,39 @@
             for y in (0, 1):
                 b2(i, d, y).wait_send()
         b3(i).wait_send()
+    for s in (5, 6, 7):
+        keep(s).wait()
+    grad_out_copy.wait()
+    block_copy.wait()
     end.wait_send()
 
 
 def block(inputs, grad_block, w_qkv, w_out):
     dma = pltpu.SemaphoreType.DMA
     anywhere = pl.BlockSpec(memory_space=pl.ANY)
-    vmem = pl.BlockSpec(memory_space=pltpu.VMEM)
     return pl.pallas_call(
         block_kernel,
         name="block",
         out_shape=(
-            jax.ShapeDtypeStruct((32, 64, 1536), BF16),
-            jax.ShapeDtypeStruct((3, 3, 8, 256, 128), BF16),
+            jax.ShapeDtypeStruct((1536, 2048), BF16),
+            jax.ShapeDtypeStruct((8, 256, 1152), BF16),
             jax.ShapeDtypeStruct((128, 1536), BF16),
             jax.ShapeDtypeStruct((3, 128, 1536), F32),
         ),
-        in_specs=[vmem, vmem, anywhere, vmem],
-        out_specs=(anywhere, anywhere, vmem, vmem),
+        in_specs=[anywhere] * 4,
+        out_specs=(anywhere,) * 4,
         scratch_shapes=[
             pltpu.VMEM((2, 32, 64, 1536), BF16),
             pltpu.VMEM((8, 4, 256, 384), BF16),
             pltpu.VMEM((8, 2, 4, 32, 384), BF16),
             pltpu.VMEM((8, 2, 4, 64, 384), BF16),
             pltpu.VMEM((8, 4, 64, 384), BF16),
+            pltpu.VMEM((max(len(across_first), 1), 3, 256, 384), BF16),
             pltpu.VMEM((8, 4, 64, 384), BF16),
             pltpu.VMEM((3, 1536, 384), BF16),
+            pltpu.VMEM((3, 128, 1536), BF16),
+            pltpu.VMEM((128, 1536), BF16),
+            pltpu.VMEM((3, 128, 1536), F32),
             pltpu.VMEM((2, 8, 256, 384), BF16),
             pltpu.VMEM((8, 256, 256), F32),
             pltpu.VMEM((8, 256, 256), F32),
@@ -766,13 +946,13 @@
             dma((2, 8, 2)), dma((2, 8, 2)),
             dma((2, 8)), dma((2, 8)),
             dma((2, 8)), dma((2, 8)),
-            dma((8,)), dma(()), dma((2,)),
+            dma((8,)), dma((2,)), dma((2,)), dma((max(len(across_first), 1),)), dma((max(len(across_first), 1),)), dma((2,)),
             dma((8, 7)), dma((8, 7)),
             dma((3,)), dma((3,)),
             dma((3, 2)), dma((3, 2)),
             dma((3, 2)), dma((3, 2)),
             dma((3, 3)), dma((3, 3)),
-            dma((3, 4, 5)), dma((3, 4, 5)),
+            dma((3, 4, 8)), dma((3, 4, 8)),
             dma((3, 4)), dma((3, 3)),
             dma((4, 2)), dma((4, 2)),
             dma((4, 2)), dma((4, 2)),
@@ -786,55 +966,76 @@
     )(inputs.reshape(2, 64, 1536), grad_block.reshape(2, 64, 1536), jnp.transpose(w_qkv, (1, 0, 2)), w_out)
 
 
-def weight_kernel(x_ref, rows_hbm, block_hbm, grad_out_hbm, out_ref, block_copy, grad_out_copy, rows, sem):
-    step = pl.program_id(0)
+def weight_kernel(x_hbm, rows_hbm, block_hbm, grad_out_hbm, out_hbm, block_copy, grad_out_copy, x, rows, out, block_rows, grad_out, x_sem, sem, out_sem):
+    def load(m):
+        features = pl.ds(m * 256, 256)
+        return pltpu.make_async_copy(x_hbm.at[features], x.at[features], x_sem.at[m])
+
+    def store(m, h):
+        return pltpu.make_async_copy(out.at[m % 2, :, h * 384:(h + 1) * 384], out_hbm.at[h, pl.ds(m * 256, 256)], out_sem.at[m, h])
+
     copies = [
-        pltpu.make_async_copy(block_hbm, block_copy, sem.at[3]),
-        pltpu.make_async_copy(grad_out_hbm, grad_out_copy, sem.at[4]),
+        pltpu.make_async_copy(rows_hbm, rows, sem.at[0]),
+        pltpu.make_async_copy(block_hbm, block_rows, sem.at[1]),
+        pltpu.make_async_copy(grad_out_hbm, grad_out, sem.at[2]),
     ]
-
-    @pl.when(step == 0)
-    def _():
-        loads = [pltpu.make_async_copy(rows_hbm.at[:, h], rows.at[h], sem.at[h]) for h in range(3)]
-        for load in loads:
-            load.start()
-        for copy in copies:
-            copy.start()
-        for load in loads:
-            load.wait()
-
-    turned = x_ref[...].reshape(2048, 256).T
-    for h in range(3):
-        factor = jnp.concatenate([rows[h, t].reshape(2048, 128) for t in range(3)], axis=1)
-        out_ref[h] = jnp.dot(turned, factor, preferred_element_type=F32)
-
-    @pl.when(step == pl.num_programs(0) - 1)
-    def _():
-        for copy in copies:
-            copy.wait()
-
-
-def weight_grad(tokens, rows, block_rows, grad_out):
+    passed_on = [
+        pltpu.make_async_copy(block_rows, block_copy, sem.at[1]),
+        pltpu.make_async_copy(grad_out, grad_out_copy, sem.at[2]),
+    ]
+    copies[0].start()
+    for m in range(6):
+        load(m).start()
+    copies[1].start()
+    copies[2].start()
+    copies[0].wait()
+    for m in range(6):
+        load(m).wait()
+        if m >= 2:
+            for h in range(3):
+                store(m - 2, h).wait()
+        out[m % 2] = jnp.dot(x[m * 256:(m + 1) * 256], rows[...].reshape(2048, 1152), preferred_element_type=F32)
+        for h in range(3):
+            store(m, h).start()
+        if m == 1:
+            for k in (1, 2):
+                copies[k].wait()
+                passed_on[k - 1].start()
+    for m in (4, 5):
+        for h in range(3):
+            store(m, h).wait()
+    for copy in passed_on:
+        copy.wait()
+
+
+def weight_grad(turned, rows, block_rows, grad_out):
+    dma = pltpu.SemaphoreType.DMA
     anywhere = pl.BlockSpec(memory_space=pl.ANY)
     return pl.pallas_call(
         weight_kernel,
         name="weight_grad",
-        grid=(6,),
         out_shape=(
             jax.ShapeDtypeStruct((3, 1536, 384), F32),
             jax.ShapeDtypeStruct((128, 1536), BF16),
             jax.ShapeDtypeStruct((3, 128, 1536), F32),
         ),
-        in_specs=[pl.BlockSpec((32, 64, 256), lambda m: (0, 0, m)), anywhere, anywhere, anywhere],
-        out_specs=(pl.BlockSpec((3, 256, 384), lambda m: (0, m, 0)), anywhere, anywhere),
-        scratch_shapes=[pltpu.VMEM((3, 3, 8, 256, 128), BF16), pltpu.SemaphoreType.DMA((5,))],
-        compiler_params=pltpu.CompilerParams(vmem_limit_bytes=48 << 20),
-    )(tokens, rows, block_rows, grad_out)
+        in_specs=[anywhere] * 4,
+        out_specs=(anywhere,) * 3,
+        scratch_shapes=[
+            pltpu.VMEM((1536, 2048), BF16),
+            pltpu.VMEM((8, 256, 1152), BF16),
+            pltpu.VMEM((2, 256, 1152), F32),
+            pltpu.VMEM((128, 1536), BF16),
+            pltpu.VMEM((3, 128, 1536), F32),
+            dma((6,)), dma((3,)), dma((6, 3)),
+        ],
+        compiler_params=pltpu.CompilerParams(vmem_limit_bytes=63 << 20),
+    )(turned, rows, block_rows, grad_out)
 
 
 def local(inputs, w_qkv, w_out, grad_block):
-    tokens, rows, block_rows, grad_out = block(inputs, grad_block, w_qkv, w_out)
-    grad_qkv, block_out, grad_out = weight_grad(tokens, rows, block_rows, grad_out)
+    turned, rows, block_rows, grad_out = block(inputs, grad_block, w_qkv, w_out)
+    grad_qkv, block_out, grad_out = weight_grad(turned, rows, block_rows, grad_out)
     return block_out, jnp.transpose(grad_qkv, (1, 0, 2)), grad_out
 
 

time: 206 us -> 191 us (0.927)
  Pallas kernels: 202 us -> 189 us
  local copies, waits for them, and re-layouts: 2.65 us -> 0 us
    pallas_call x1, Pallas kernels: 185 us -> 175 us  [block(): pl.pallas_call(block_kernel, name='block', out_shape=(jax.ShapeDtypeStruc...]
    pallas_call x1, Pallas kernels: 16.9 us -> 13.7 us  [weight_grad(): pl.pallas_call(weight_kernel, name='weight_grad', out_shape=(jax.ShapeDty...]
    unnamed x4 -> x0, local copies, waits for them, and re-layouts: 2.65 us -> none
where the time goes in v3:
time: 191 us; the launch traced here: 190 us
  Pallas kernels  189 us (99%)
    pallas_call x1, Pallas kernels, block(): pl.pallas_call(block_kernel, name='block', out_shape=(jax.ShapeDtypeStruc...  175 us
    pallas_call x1, Pallas kernels, weight_grad(): pl.pallas_call(weight_kernel, name='weight_grad', out_shape=(jax.ShapeDty...  13.7 us

profile of v3, /device:TPU:17, one launch (start us, length us, event | category | flops | bytes accessed | tf_op | source)
XLA Modules:
  0.0 189.8 jit_solution(902009938696455409)
XLA Ops:
  0.6 175.3 %block.1 = (bf16[1536,2048]{1,0:T(8,128)(2,1)}, bf16[8,256,1152]{2,1,0:T(8,128)(2,1)}, bf16[128,1536]{1,0:T(8,128)(2,1)}, f32[3,128,1536]{2,1,0:T(8,128)}) custom-call(bf16[2,64,1536]{2,1,0:T(8,128)(2,1)} %bitcast.5, bf16[2,64,1536]{2,1,0:T(8,128)(2,1)} %bitcast.6, bf16[3,1536,384]{2,1,0:T(8,128)(2,1)} %bitcast.4, bf16[3,128,1536]{2,1,0:T(8,128)(2,1)} %wo_hbm.1), custom_call_target="tpu_custom_call" | custom-call | tf_op jit(solution)/shard_map/block/pallas_call | solution.py:906
  175.9 13.7 %weight_grad.1 = (f32[3,1536,384]{2,1,0:T(8,128)}, bf16[128,1536]{1,0:T(8,128)(2,1)}, f32[3,128,1536]{2,1,0:T(8,128)}) custom-call(bf16[1536,2048]{1,0:T(8,128)(2,1)} %get-tuple-element.10.x_hbm, bf16[8,256,1152]{2,1,0:T(8,128)(2,1)} %get-tuple-element.11.rows_hbm, bf16[128,1536]{1,0:T(8,128)(2,1)} %get-tuple-element.12.block_hbm, ...), custom_call_target="tpu_custom_call" | custom-call | tf_op jit(solution)/shard_map/weight_grad/pallas_call | solution.py:1014

commit v4 on v3

--- a/solution.py
+++ b/solution.py
@@ -45,16 +45,15 @@
 
 slice_at = (0, -1, 1, 2)
 along_x_first = (1,)
-across_first = ()
 
 
 def block_kernel(
     x_hbm, g_hbm, w_hbm, wo_hbm,
     turned_out, grads_out, block_hbm, grad_out_hbm,
-    held, part, relay, near, far, crossed, total, w_ref, wo_ref, block_out, grad_out,
+    held, part, relay, near, far, total, w_ref, wo_ref, block_out, grad_out,
     kv, scores, slopes, grads, twin_grads, grads_relay, grads_near, result,
     wide, turned, block_relay, block_near, block_far, final, theirs,
-    ag_send, ag_recv, s1_send, s1_recv, s2_send, s2_recv, s3_send, s3_recv, s4_send, s4_recv, x_sem, w_sem, own_sem, cross_send, cross_recv, last_sem,
+    ag_send, ag_recv, s1_send, s1_recv, s2_send, s2_recv, s3_send, s3_recv, s4_send, s4_recv, x_sem, w_sem, own_sem, last_sem,
     kv_send, kv_recv, tw_send, tw_recv, g1_send, g1_recv, g2_send, g2_recv, up_send, up_recv,
     wide_send, wide_recv, here_sem, out_sem, b0_send, b0_recv, b1_send, b1_recv, b2_send, b2_recv, b3_send, b3_recv,
     end_send, end_recv,
@@ -162,13 +161,6 @@
         ref = total.at[block_of(s), unit(a)]
         return remote(ref, ref, s4_send.at[a, s], s4_recv.at[a, s], twin)
 
-    def is_crossed(a, steps):
-        return a == 0 and steps[0] in across_first
-
-    def cross(s):
-        return remote(part.at[s, unit(0)], crossed.at[s - min(across_first)],
-                      cross_send.at[s - min(across_first)], cross_recv.at[s - min(across_first)], across)
-
     def each(steps, body):
         lo, hi = steps
         if hi - lo == 1:
@@ -191,23 +183,9 @@
                     rows[...].reshape(256, 1536), wo_ref[...].reshape(384, 1536),
                     (((1,), (1,)), ((), ())), preferred_element_type=F32,
                 ).astype(BF16)
-            if is_crossed(a, steps):
-                pl.when(is_away)(lambda: cross(s).start())
-            else:
-                for d in (0, 1):
-                    rs1(a, s, d).start()
+            for d in (0, 1):
+                rs1(a, s, d).start()
         each(steps, body)
-
-    def add_crossed(*steps):
-        @pl.when(is_home)
-        def _():
-            def body(s):
-                cross(s).wait_recv()
-                for h in range(3):
-                    add(part.at[s, h], crossed[s - min(across_first), h])
-                for d in (0, 1):
-                    rs1(0, s, d).start()
-            each(steps, body)
 
     def add(ref, *terms):
         value = ref[...].astype(F32)
@@ -222,22 +200,15 @@
                 rows = pl.ds(pl.multiple_of(me.col_x((1, -1)[d]) * 64 + 32 * d, 32), 32)
                 add(part.at[s, unit(a), rows], relay[s, d, unit(a)])
                 rs2(a, s, d).start()
-        if is_crossed(a, steps):
-            pl.when(is_home)(lambda: each(steps, body))
-        else:
-            each(steps, body)
+        each(steps, body)
 
     def add_near(a, *steps):
         def body(s):
             for d in (0, 1):
                 rs2(a, s, d).wait_recv()
             add(part.at[s, unit(a), own()], near[s, 0, unit(a)], near[s, 1, unit(a)])
-            if not is_crossed(a, steps):
-                pl.when(is_away)(lambda: rs3(a, s).start())
-        if is_crossed(a, steps):
-            pl.when(is_home)(lambda: each(steps, body))
-        else:
-            each(steps, body)
+            pl.when(is_away)(lambda: rs3(a, s).start())
+        each(steps, body)
 
     def kv_gather(s, k):
         x, rows, device = {
@@ -263,13 +234,10 @@
 
             @pl.when(is_home)
             def _():
-                if is_crossed(a, steps):
-                    total[block, unit(a)] = part[s, unit(a), own()]
-                else:
-                    rs3(a, s).wait_recv()
-                    total[block, unit(a)] = (
-                        part[s, unit(a), own()].astype(F32) + far[s, unit(a)].astype(F32)
-                    ).astype(BF16)
+                rs3(a, s).wait_recv()
+                total[block, unit(a)] = (
+                    part[s, unit(a), own()].astype(F32) + far[s, unit(a)].astype(F32)
+                ).astype(BF16)
                 rs4(a, s).start()
 
             @pl.when(is_away)
@@ -305,15 +273,33 @@
                 kv_gather(s, k).wait_recv()
         each(steps, body)
 
-    def attend(h):
-        query = total[:, h, my_rows, 0:128].reshape(256, 128)
-        cotangent = total[:, 3, my_rows, h * 128:(h + 1) * 128].reshape(256, 128)
-        transposed = (((1,), (1,)), ((), ()))
-        first = (((0,), (0,)), ((), ()))
+    def part_free():
+        for s in range(8):
+            for d in (0, 1):
+                rs1(0, s, d).wait_send()
+                rs2(0, s, d).wait_send()
+
+            @pl.when(is_away)
+            def _():
+                rs3(0, s).wait_send()
+
+    transposed = (((1,), (1,)), ((), ()))
+    by_rows = (((0,), (0,)), ((), ()))
+
+    def query_of(h):
+        return total[:, h, my_rows, 0:128].reshape(256, 128)
+
+    def write_rows(t, h, low_half, high_half):
+        rows = jnp.concatenate([low_half[:, :128], high_half], axis=1).T.astype(BF16)
+        result[t, h, :, my_rows] = rows.reshape(8, 32, 128)
+
+    def attend_forward(h):
+        query = query_of(h)
+        head = slice(h * 128, (h + 1) * 128)
 
         def masked(b, lanes):
             width = 256 - lanes
-            s = lax.dot_general(kv[0, b, :, h * 128:(h + 1) * 128], query[lanes:], transposed, preferred_element_type=F32) * scale
+            s = lax.dot_general(kv[0, b, :, head], query[lanes:], transposed, preferred_element_type=F32) * scale
             key_at = b * 256 + lax.broadcasted_iota(jnp.int32, (256, width), 0)
             column = lanes + lax.broadcasted_iota(jnp.int32, (1, width), 1)
             query_at = (column // 32) * 256 + me.x * 64 + me.core * 32 + column % 32
@@ -326,47 +312,63 @@
                 return jnp.maximum(m, jnp.max(s, axis=0, keepdims=True))
             return body
 
-        m = lax.fori_loop(0, 4, top(0), jnp.full((1, 256), fill, F32))
-        m_high = lax.fori_loop(4, 8, top(128), m[:, 128:])
+        m = lax.fori_loop(0, 4, top(0), jnp.full((1, 256), fill, F32), unroll=True)
+        m_high = lax.fori_loop(4, 8, top(128), m[:, 128:], unroll=True)
         m = jnp.concatenate([m[:, :128], m_high], axis=1)
 
         def sums(lanes, m):
-            def body(b, carry):
-                norm, slope = carry
+            def body(b, norm):
                 e = jnp.exp(scores[b, :, lanes:] - m)
                 scores[b, :, lanes:] = e
-                dp = lax.dot_general(kv[1, b, :, h * 128:(h + 1) * 128], cotangent[lanes:], transposed, preferred_element_type=F32)
+                return norm + jnp.sum(e, axis=0, keepdims=True)
+            return body
+
+        norm = lax.fori_loop(0, 4, sums(0, m), jnp.zeros((1, 256), F32), unroll=True)
+        norm_high = lax.fori_loop(4, 8, sums(128, m_high), norm[:, 128:], unroll=True)
+        inverse = 1.0 / jnp.concatenate([norm[:, :128], norm_high], axis=1)
+
+        def rows(lanes):
+            def body(b, att):
+                w = (scores[b, :, lanes:] * inverse[:, lanes:]).astype(BF16)
+                part[b, h, :, lanes:256] = w
+                return att + lax.dot_general(kv[1, b, :, head], w, by_rows, preferred_element_type=F32)
+            return body
+
+        att = lax.fori_loop(0, 4, rows(0), jnp.zeros((128, 256), F32), unroll=True)
+        att_high = lax.fori_loop(4, 8, rows(128), att[:, 128:], unroll=True)
+        write_rows(0, h, att, att_high)
+        pl.when(is_away)(lambda: lift(h, 0).start())
+
+    def attend_backward(h):
+        query = query_of(h)
+        head = slice(h * 128, (h + 1) * 128)
+        cotangent = total[:, 3, my_rows, head].reshape(256, 128)
+
+        def sums(lanes):
+            def body(b, slope):
+                dp = lax.dot_general(kv[1, b, :, head], cotangent[lanes:], transposed, preferred_element_type=F32)
                 slopes[b, :, lanes:] = dp
-                return (norm + jnp.sum(e, axis=0, keepdims=True), slope + jnp.sum(e * dp, axis=0, keepdims=True))
+                return slope + jnp.sum(part[b, h, :, lanes:256].astype(F32) * dp, axis=0, keepdims=True)
             return body
 
-        zero = jnp.zeros((1, 256), F32)
-        norm, slope = lax.fori_loop(0, 4, sums(0, m), (zero, zero))
-        norm_high, slope_high = lax.fori_loop(4, 8, sums(128, m_high), (norm[:, 128:], slope[:, 128:]))
-        norm = jnp.concatenate([norm[:, :128], norm_high], axis=1)
+        slope = lax.fori_loop(0, 4, sums(0), jnp.zeros((1, 256), F32), unroll=True)
+        slope_high = lax.fori_loop(4, 8, sums(128), slope[:, 128:], unroll=True)
         slope = jnp.concatenate([slope[:, :128], slope_high], axis=1)
-        inverse = 1.0 / norm
-        slope = slope * inverse
-
-        def backward(lanes):
-            def body(b, carry):
-                att, dq = carry
-                p = scores[b, :, lanes:] * inverse[:, lanes:]
-                w = p.astype(BF16)
-                ds = (p * (slopes[b, :, lanes:] - slope[:, lanes:]) * scale).astype(BF16)
+
+        def terms(lanes):
+            def body(b, dq):
+                w = part[b, h, :, lanes:256]
+                ds = (w.astype(F32) * (slopes[b, :, lanes:] - slope[:, lanes:]) * scale).astype(BF16)
                 grads[h, 0, b] = jnp.dot(ds, query[lanes:], preferred_element_type=F32).astype(BF16)
                 grads[h, 1, b] = jnp.dot(w, cotangent[lanes:], preferred_element_type=F32).astype(BF16)
-                att = att + lax.dot_general(kv[1, b, :, h * 128:(h + 1) * 128], w, first, preferred_element_type=F32)
-                dq = dq + lax.dot_general(kv[0, b, :, h * 128:(h + 1) * 128], ds, first, preferred_element_type=F32)
-                return att, dq
+                return dq + lax.dot_general(kv[0, b, :, head], ds, by_rows, preferred_element_type=F32)
             return body
 
-        square = jnp.zeros((128, 256), F32)
-        att, dq = lax.fori_loop(0, 4, backward(0), (square, square))
-        att_high, dq_high = lax.fori_loop(4, 8, backward(128), (att[:, 128:], dq[:, 128:]))
-        for t, lo, hi in ((0, att, att_high), (1, dq, dq_high)):
-            rows = jnp.concatenate([lo[:, :128], hi], axis=1).T.astype(BF16)
-            result[t, h, :, my_rows] = rows.reshape(8, 32, 128)
+        dq = lax.fori_loop(0, 4, terms(0), jnp.zeros((128, 256), F32), unroll=True)
+        dq_high = lax.fori_loop(4, 8, terms(128), dq[:, 128:], unroll=True)
+        write_rows(1, h, dq, dq_high)
+        to_twin(h).start()
+        pl.when(is_away)(lambda: lift(h, 1).start())
 
     def to_twin(h):
         return remote(grads.at[h, 1 - me.core], twin_grads.at[h], tw_send.at[h], tw_recv.at[h], twin)
@@ -416,14 +418,6 @@
     def lifted(h, t):
         ref = result.at[t, h, every, their_rows] if t < 2 else result.at[3 - me.core, h]
         remote(ref, ref, up_send.at[h, t], up_recv.at[h, t], twin).wait_recv()
-
-    def after(h):
-        to_twin(h).start()
-
-        @pl.when(is_away)
-        def _():
-            lift(h, 0).start()
-            lift(h, 1).start()
 
     def spread(h, t, k):
         x, blocks, device = {
@@ -603,216 +597,218 @@
 
     own_copy[0].wait()
     go(0, 9, 0, 1, 2)
-    w_copy.wait()
-    work(0, 0, 1)
     own_copy[1].wait()
     go(1, 9)
     wo_copy.wait()
     work(1, 0, 1)
+    w_copy.wait()
+    work(0, 0, 1)
     add_relay(0, 0, 1)
     landed(0, 0)
     go(0, 3, 4, 10)
-    add_relay(1, 0, 1)
     landed(0, 2)
     go(0, 6, 12)
-    work(0, 1, 2)
     landed(0, 1)
     go(0, 5, 11)
+    add_relay(1, 0, 1)
+    work(0, 1, 4)
+    add_relay(0, 2, 3)
     add_near(0, 0, 1)
-    work(0, 2, 4)
+    landed(0, 4)
+    go(0, 8, 14)
     add_relay(0, 1, 2)
+    go(1, 0)
     add_relay(0, 3, 4)
-    go(1, 1, 2)
     landed(0, 3)
     go(0, 7, 13)
-    add_relay(0, 2, 3)
+    work(0, 4, 5)
+    go(1, 1, 2)
+    add_near(1, 0, 1)
+    work(0, 5, 6)
+    add_far(0, 0, 1)
     landed(0, 5, 6)
     go(0, 15)
-    landed(0, 4)
-    go(0, 8, 14)
-    go(1, 0)
-    work(0, 4, 6)
-    add_near(0, 3, 4)
-    add_far(0, 0, 1)
-    work(0, 6, 7)
-    add_near(0, 1, 2)
-    add_relay(0, 4, 5)
-    kv_relay(0, 1)
     landed(0, 7, 8)
     go(0, 16)
-    add_near(0, 2, 3)
+    work(0, 6, 7)
+    add_near(0, 3, 4)
     landed(1, 0)
     go(1, 3, 4, 10)
+    work(0, 7, 8)
+    add_relay(0, 4, 5)
+    work(1, 1, 2)
+    add_far(0, 3, 4)
+    add_near(0, 1, 2)
+    add_relay(0, 5, 6)
+    add_near(0, 4, 5)
+    add_relay(0, 6, 7)
+    kv_relay(3, 4)
+    add_far(1, 0, 1)
+    kv_relay(0, 1)
+    turn(0, 1)
+    landed(1, 1)
+    go(1, 5, 11)
+    add_far(0, 1, 2)
     landed(1, 2)
     go(1, 6, 12)
-    landed(1, 1)
-    go(1, 5, 11)
-    add_far(0, 3, 4)
-    add_far(0, 1, 2)
-    add_near(1, 0, 1)
-    add_relay(0, 5, 6)
-    add_near(0, 4, 5)
-    work(1, 1, 2)
-    work(0, 7, 8)
-    add_relay(0, 6, 7)
-    work(1, 3, 4)
+    add_near(0, 5, 6)
+    add_near(0, 2, 3)
+    landed(1, 3)
+    go(1, 7, 13)
+    add_far(0, 4, 5)
+    work(1, 2, 3)
     landed(1, 4)
     go(1, 8, 14)
-    landed(1, 3)
-    go(1, 7, 13)
     add_relay(0, 7, 8)
-    add_far(0, 2, 3)
-    add_far(0, 4, 5)
-    add_near(0, 5, 6)
-    kv_relay(2, 3)
+    work(1, 3, 4)
+    work(1, 5, 6)
     landed(1, 5, 6)
     go(1, 15)
-    add_relay(1, 1, 2)
-    kv_relay(3, 4)
+    add_far(0, 5, 6)
+    add_near(0, 6, 8)
+    add_far(0, 2, 3)
     kv_relay(1, 2)
-    work(1, 2, 3)
-    work(1, 5, 6)
-    add_near(0, 7, 8)
-    add_far(0, 5, 6)
-    add_relay(1, 2, 3)
-    kv_done(1, 2)
-    add_near(0, 6, 7)
-    work(1, 4, 5)
     kv_relay(4, 5)
     landed(1, 7, 8)
     go(1, 16)
+    add_relay(1, 1, 3)
+    work(1, 6, 7)
+    work(1, 4, 5)
+    kv_done(3, 4)
     add_near(1, 1, 2)
-    kv_relay(5, 6)
-    kv_done(2, 3)
-    add_relay(1, 3, 4)
+    kv_done(1, 2)
+    kv_done(4, 5)
     add_relay(1, 5, 6)
-    kv_done(4, 5)
-    kv_done(3, 4)
-    work(1, 6, 7)
-    kv_done(5, 6)
-    add_far(0, 7, 8)
-    add_far(1, 0, 1)
-    kv_whole(4, 5)
-    add_relay(1, 4, 5)
-    add_near(1, 3, 4)
     work(1, 7, 8)
     kv_done(0, 1)
+    kv_relay(2, 3)
+    add_relay(1, 6, 7)
+    add_relay(1, 3, 4)
+    add_near(1, 2, 3)
+    add_relay(1, 4, 5)
     add_near(1, 5, 6)
-    add_relay(1, 6, 7)
-    add_near(1, 2, 3)
+    turn(1, 2)
+    add_far(0, 7, 8)
+    kv_whole(0, 1)
+    add_relay(1, 7, 8)
+    add_near(1, 3, 4)
+    add_far(1, 1, 2)
+    kv_done(2, 3)
     add_far(0, 6, 7)
-    turn(0, 1)
-    add_far(1, 1, 2)
-    turn(1, 2)
-    add_relay(1, 7, 8)
-    kv_whole(0, 1)
+    add_far(1, 2, 3)
     add_near(1, 4, 5)
     add_near(1, 6, 7)
-    kv_relay(6, 8)
-    kv_whole(2, 3)
+    kv_relay(7, 8)
+    add_far(1, 5, 6)
+    kv_relay(5, 6)
+    kv_whole(1, 2)
     add_near(1, 7, 8)
+    kv_whole(4, 5)
+    kv_whole(3, 4)
+    kv_relay(6, 7)
+    kv_done(7, 8)
+    turn(2, 3)
+    kv_done(5, 6)
     add_far(1, 3, 4)
     kv_done(6, 7)
-    add_far(1, 2, 3)
-    kv_whole(1, 2)
-    add_far(1, 5, 6)
-    kv_done(7, 8)
+    kv_whole(2, 3)
     add_far(1, 6, 7)
+    kv_whole(7, 8)
     add_far(1, 4, 5)
     add_far(1, 7, 8)
-    kv_whole(3, 4)
-    kv_whole(6, 8)
-    kv_whole(5, 6)
-    attend(0)
-    after(0)
+    kv_whole(5, 7)
+    part_free()
+    attend_forward(0)
+    attend_backward(0)
     spread_home(0, (0,))
+    attend_forward(1)
+    spread_away(0, (0,))
+    add_twin(0)
+    attend_backward(1)
     spread_home(0, (1,))
-    add_twin(0)
-    attend(1)
     add_grads_relay(0)
-    after(1)
+    turn(3, 4)
+    attend_forward(2)
+    spread_away(0, (1,))
+    spread_home(1, (1,))
     spread_home(1, (0,))
-    spread_home(1, (1,))
-    spread_away(0, (1,))
-    attend(2)
-    after(2)
+    attend_backward(2)
     spread_home(2, (0,))
+    spread_away(1, (0,))
+    spread_away(2, (0,))
+    spread_away(1, (1,))
     add_twin(1)
-    spread_away(0, (0,))
-    spread_away(1, (1,))
-    spread_away(1, (0,))
+    spread_relay(0, (1,))
+    turn(4, 5)
+    turn(5, 6)
+    spread_home(2, (1,))
+    spread_away(2, (1,))
+    add_twin(2)
     add_grads_near(0)
-    spread_relay(1, (0,))
-    turn(2, 3)
-    spread_home(2, (1,))
-    turn(3, 4)
-    turn(4, 5)
-    spread_away(2, (0,))
-    spread_relay(0, (1,))
-    turn(5, 6)
+    add_grads_relay(1)
     turn(6, 7)
     turn(7, 8)
-    add_twin(2)
+    spread_relay(0, (0,))
     spread_relay(1, (1,))
-    add_grads_relay(1)
-    spread_away(2, (1,))
     for k in range(17):
         gather(0, k).wait_send()
     multiply_out(0)
     spread_relay(2, (1,))
     add_grads_near(1)
+    add_grads_relay(2)
+    spread_relay(1, (0,))
     spread_home(0, (2,))
     spread_relay(2, (0,))
-    spread_relay(0, (0,))
+    spread_home(0, (3,))
     add_block_twin(0)
-    add_grads_relay(2)
+    spread_away(0, (2,))
     multiply_out(1)
     add_block_relay(0)
+    multiply_out(2)
+    add_block_twin(1)
     spread_home(1, (2,))
-    spread_home(1, (3,))
-    multiply_out(2)
+    spread_done(0, (0,))
     spread_done(1, (0,))
-    spread_home(0, (3,))
-    add_block_twin(1)
+    spread_away(0, (3,))
     add_grads_near(2)
-    spread_home(2, (2,))
-    spread_home(2, (3,))
-    spread_done(0, (0,))
-    spread_away(0, (2,))
     add_block_twin(2)
     spread_away(1, (2,))
+    spread_relay(0, (2,))
+    add_block_near(0)
+    add_block_relay(1)
+    spread_done(1, (1,))
+    spread_home(2, (2,))
+    spread_relay(0, (3,))
+    add_block_relay(2)
+    spread_home(2, (3,))
     spread_done(2, (0,))
-    spread_away(0, (3,))
-    add_block_near(0)
-    spread_away(1, (3,))
-    spread_done(1, (1,))
-    spread_away(2, (2,))
-    add_block_relay(1)
-    spread_away(2, (3,))
-    add_block_relay(2)
     multiply_out(3)
     grad_out_copy = pltpu.make_async_copy(grad_out, grad_out_hbm, last_sem.at[0])
     grad_out_copy.start()
+    spread_home(1, (3,))
+    add_block_far(0)
+    add_block_near(1)
+    spread_away(2, (2,))
+    spread_away(2, (3,))
+    spread_away(1, (3,))
+    spread_relay(1, (2,))
+    spread_done(0, (3,))
+    spread_done(0, (2,))
+    add_block_twin(3)
     spread_done(2, (1,))
-    spread_relay(0, (3,))
-    add_block_twin(3)
-    add_block_near(1)
-    spread_relay(2, (3,))
-    spread_relay(1, (2,))
     add_block_near(2)
-    spread_relay(0, (2,))
     add_block_relay(3)
     spread_done(0, (1,))
+    spread_relay(2, (2,))
+    spread_relay(2, (3,))
+    add_block_far(2)
     spread_relay(1, (3,))
+    spread_done(1, (2,))
     add_block_near(3)
     spread_done(2, (3,))
-    add_block_far(2)
-    spread_relay(2, (2,))
-    spread_done(1, (2,))
-    add_block_far(0)
     spread_done(2, (2,))
-    spread_done(0, (2,))
     add_block_far(1)
+    spread_done(1, (3,))
     add_block_far(3)
     their_half = pl.ds(pl.multiple_of(128 - me.core * 128, 128), 128)
     end = remote(final.at[their_half], theirs, end_send, end_recv, twin)
@@ -832,23 +828,10 @@
 
     block_copy = pltpu.make_async_copy(block_out, block_hbm, last_sem.at[1])
     block_copy.start()
-    spread_done(0, (3,))
-    spread_done(1, (3,))
-
-    def sums_sent(a, s):
-        for d in (0, 1):
-            rs1(a, s, d).wait_send()
-            rs2(a, s, d).wait_send()
 
     @pl.when(is_away)
     def _():
-        for s in range(8):
-            for a in (0, 1):
-                if a == 0 and s in across_first:
-                    cross(s).wait_send()
-                else:
-                    rs3(a, s).wait_send()
-                    sums_sent(a, s)
+        pl.loop(0, 8)(lambda s: rs3(1, s).wait_send())
         for h in range(3):
             for t in range(3):
                 lift(h, t).wait_send()
@@ -859,7 +842,6 @@
             @pl.loop(0, 8)
             def _(s):
                 rs4(a, s).wait_send()
-                sums_sent(a, s)
         for h in range(3):
             for t in range(4):
                 spread(h, t, 0).wait_send()
@@ -872,6 +854,9 @@
 
     @pl.loop(0, 8)
     def _(s):
+        for d in (0, 1):
+            rs1(1, s, d).wait_send()
+            rs2(1, s, d).wait_send()
         for k in range(7):
             kv_gather(s, k).wait_send()
 
@@ -920,7 +905,6 @@
             pltpu.VMEM((8, 2, 4, 32, 384), BF16),
             pltpu.VMEM((8, 2, 4, 64, 384), BF16),
             pltpu.VMEM((8, 4, 64, 384), BF16),
-            pltpu.VMEM((max(len(across_first), 1), 3, 256, 384), BF16),
             pltpu.VMEM((8, 4, 64, 384), BF16),
             pltpu.VMEM((3, 1536, 384), BF16),
             pltpu.VMEM((3, 128, 1536), BF16),
@@ -946,7 +930,7 @@
             dma((2, 8, 2)), dma((2, 8, 2)),
             dma((2, 8)), dma((2, 8)),
             dma((2, 8)), dma((2, 8)),
-            dma((8,)), dma((2,)), dma((2,)), dma((max(len(across_first), 1),)), dma((max(len(across_first), 1),)), dma((2,)),
+            dma((8,)), dma((2,)), dma((2,)), dma((2,)),
             dma((8, 7)), dma((8, 7)),
             dma((3,)), dma((3,)),
             dma((3, 2)), dma((3, 2)),

time: 191 us -> 178 us (0.932)
  Pallas kernels: 189 us -> 178 us
    pallas_call x1, Pallas kernels: 175 us -> 164 us  [block(): pl.pallas_call(block_kernel, name='block', out_shape=(jax.ShapeDtypeStruc...]
where the time goes in v4:
time: 178 us
  Pallas kernels  178 us (100%)
    pallas_call x1, Pallas kernels, block(): pl.pallas_call(block_kernel, name='block', out_shape=(jax.ShapeDtypeStruc...  164 us
    pallas_call x1, Pallas kernels, weight_grad(): pl.pallas_call(weight_kernel, name='weight_grad', out_shape=(jax.ShapeDty...  13.7 us

profile of v4, /device:TPU:17, one launch (start us, length us, event | category | flops | bytes accessed | tf_op | source)
XLA Modules:
  0.0 178.3 jit_solution(9646099786921258185)
XLA Ops:
  0.6 163.8 %block.1 = (bf16[1536,2048]{1,0:T(8,128)(2,1)}, bf16[8,256,1152]{2,1,0:T(8,128)(2,1)}, bf16[128,1536]{1,0:T(8,128)(2,1)}, f32[3,128,1536]{2,1,0:T(8,128)}) custom-call(bf16[2,64,1536]{2,1,0:T(8,128)(2,1)} %bitcast.5, bf16[2,64,1536]{2,1,0:T(8,128)(2,1)} %bitcast.6, bf16[3,1536,384]{2,1,0:T(8,128)(2,1)} %bitcast.4, bf16[3,128,1536]{2,1,0:T(8,128)(2,1)} %wo_hbm.1), custom_call_target="tpu_custom_call" | custom-call | tf_op jit(solution)/shard_map/block/pallas_call | solution.py:891
  164.4 13.7 %weight_grad.1 = (f32[3,1536,384]{2,1,0:T(8,128)}, bf16[128,1536]{1,0:T(8,128)(2,1)}, f32[3,128,1536]{2,1,0:T(8,128)}) custom-call(bf16[1536,2048]{1,0:T(8,128)(2,1)} %get-tuple-element.10.x_hbm, bf16[8,256,1152]{2,1,0:T(8,128)(2,1)} %get-tuple-element.11.rows_hbm, bf16[128,1536]{1,0:T(8,128)(2,1)} %get-tuple-element.12.block_hbm, ...), custom_call_target="tpu_custom_call" | custom-call | tf_op jit(solution)/shard_map/weight_grad/pallas_call | solution.py:998

commit v5 on v4

--- a/solution.py
+++ b/solution.py
@@ -76,10 +76,11 @@
         pltpu.make_async_copy(ref, held.at[a, pl.ds(me.slot() * 2, 2)], own_sem.at[a])
         for a, ref in enumerate((x_hbm, g_hbm))
     ]
-    w_copy = pltpu.make_async_copy(w_hbm, w_ref, w_sem.at[0])
-    wo_copy = pltpu.make_async_copy(wo_hbm, wo_ref, w_sem.at[1])
+    w_copy = [pltpu.make_async_copy(w_hbm.at[h], w_ref.at[:, h * 384:(h + 1) * 384], w_sem.at[h]) for h in range(3)]
+    wo_copy = pltpu.make_async_copy(wo_hbm, wo_ref, w_sem.at[3])
     own_copy[0].start()
-    w_copy.start()
+    for copy in w_copy:
+        copy.start()
     own_copy[1].start()
     wo_copy.start()
     meet([beside, up, down, twin, right, left, across])
@@ -131,18 +132,16 @@
 
     def keep(s):
         columns = pl.ds(pl.multiple_of(block_of(s) * 256, 256), 256)
-        return pltpu.make_async_copy(w_ref.at[s % 3, :, 0:256], turned_out.at[:, columns], x_sem.at[s])
+        return pltpu.make_async_copy(w_ref.at[:, s % 4 * 256:s % 4 * 256 + 256], turned_out.at[:, columns], x_sem.at[s])
 
     def turn(*steps):
         for s in range(*steps):
-            if s >= 3:
-                keep(s - 3).wait()
-
-            @pl.loop(0, 12)
-            def _(n):
-                lanes = pl.ds(pl.multiple_of(n * 128, 128), 128)
+            if s >= 4:
+                keep(s - 4).wait()
+            for n in range(12):
+                lanes = slice(n * 128, (n + 1) * 128)
                 rows = held[0, pl.ds(block_of(s) * 4, 4), :, lanes].reshape(256, 128)
-                w_ref[s % 3, lanes, 0:256] = rows.T
+                w_ref[lanes, s % 4 * 256:s % 4 * 256 + 256] = rows.T
 
             keep(s).start()
 
@@ -173,11 +172,11 @@
             remote(held.at[a, pl.ds(0, 2)], held.at[a, pl.ds(0, 2)], ag_send.at[a, 9 + s], ag_recv.at[a, 9 + s], twin).wait_recv()
             rows = held.at[a, pl.ds(block_of(s) * 4, 4)]
             if a == 0:
-                @pl.loop(0, 3)
-                def _(h):
-                    part[s, h] = jnp.dot(
-                        rows[...].reshape(256, 1536), w_ref[h], preferred_element_type=F32
-                    ).astype(BF16)
+                product = jnp.dot(
+                    rows[...].reshape(256, 1536), w_ref[...], preferred_element_type=F32
+                ).astype(BF16)
+                for h in range(3):
+                    part[s, h] = product[:, h * 384:(h + 1) * 384]
             else:
                 part[s, 3] = lax.dot_general(
                     rows[...].reshape(256, 1536), wo_ref[...].reshape(384, 1536),
@@ -542,23 +541,19 @@
         mine = jnp.concatenate([wide[0, h, :, own(slice_at[i])].reshape(512, 128) for h in range(3)], axis=1)
         turned[...] = mine.T
 
-        @pl.loop(0, 4)
-        def _(n):
-            lanes = pl.ds(pl.multiple_of(n * 384, 384), 384)
+        for n in (0, 1):
+            lanes = slice(n * 768, (n + 1) * 768)
             held[0, pl.ds(i * 8, 8), :, lanes] = jnp.dot(
-                mine, wo_ref[:, :, lanes].reshape(384, 384), preferred_element_type=F32
-            ).astype(BF16).reshape(8, 64, 384)
-
+                mine, wo_ref[:, :, lanes].reshape(384, 768), preferred_element_type=F32
+            ).astype(BF16).reshape(8, 64, 768)
         b0(i, 0).start()
         b0(i, 1).start()
-
-        @pl.loop(0, 4)
-        def _(n):
-            lanes = pl.ds(pl.multiple_of(n * 384, 384), 384)
+        for n in (0, 1):
+            lanes = slice(n * 768, (n + 1) * 768)
             tokens = [held[1, b * 4 + me.col_x(slice_at[i]), :, lanes] for b in range(8)]
             term = jnp.dot(
                 turned[...], jnp.concatenate(tokens, axis=0), preferred_element_type=F32
-            ).reshape(3, 128, 384)
+            ).reshape(3, 128, 768)
             if i == 0:
                 grad_out[:, :, lanes] = term
             else:
@@ -601,7 +596,8 @@
     go(1, 9)
     wo_copy.wait()
     work(1, 0, 1)
-    w_copy.wait()
+    for copy in w_copy:
+        copy.wait()
     work(0, 0, 1)
     add_relay(0, 0, 1)
     landed(0, 0)
@@ -878,7 +874,7 @@
             for y in (0, 1):
                 b2(i, d, y).wait_send()
         b3(i).wait_send()
-    for s in (5, 6, 7):
+    for s in (4, 5, 6, 7):
         keep(s).wait()
     grad_out_copy.wait()
     block_copy.wait()
@@ -906,7 +902,7 @@
             pltpu.VMEM((8, 2, 4, 64, 384), BF16),
             pltpu.VMEM((8, 4, 64, 384), BF16),
             pltpu.VMEM((8, 4, 64, 384), BF16),
-            pltpu.VMEM((3, 1536, 384), BF16),
+            pltpu.VMEM((1536, 1152), BF16),
             pltpu.VMEM((3, 128, 1536), BF16),
             pltpu.VMEM((128, 1536), BF16),
             pltpu.VMEM((3, 128, 1536), F32),
@@ -930,7 +926,7 @@
             dma((2, 8, 2)), dma((2, 8, 2)),
             dma((2, 8)), dma((2, 8)),
             dma((2, 8)), dma((2, 8)),
-            dma((8,)), dma((2,)), dma((2,)), dma((2,)),
+            dma((8,)), dma((4,)), dma((2,)), dma((2,)),
             dma((8, 7)), dma((8, 7)),
             dma((3,)), dma((3,)),
             dma((3, 2)), dma((3, 2)),

time: 178 us -> 173 us (0.972)
  Pallas kernels: 178 us -> 173 us
    pallas_call x1, Pallas kernels: 164 us -> 159 us  [block(): pl.pallas_call(block_kernel, name='block', out_shape=(jax.ShapeDtypeStruc...]
where the time goes in v5:
time: 173 us
  Pallas kernels  173 us (100%)
    pallas_call x1, Pallas kernels, block(): pl.pallas_call(block_kernel, name='block', out_shape=(jax.ShapeDtypeStruc...  159 us
    pallas_call x1, Pallas kernels, weight_grad(): pl.pallas_call(weight_kernel, name='weight_grad', out_shape=(jax.ShapeDty...  13.7 us

profile of v5, /device:TPU:17, one launch (start us, length us, event | category | flops | bytes accessed | tf_op | source)
XLA Modules:
  0.0 173.4 jit_solution(13429525739921730167)
XLA Ops:
  0.6 158.8 %block.1 = (bf16[1536,2048]{1,0:T(8,128)(2,1)}, bf16[8,256,1152]{2,1,0:T(8,128)(2,1)}, bf16[128,1536]{1,0:T(8,128)(2,1)}, f32[3,128,1536]{2,1,0:T(8,128)}) custom-call(bf16[2,64,1536]{2,1,0:T(8,128)(2,1)} %bitcast.5, bf16[2,64,1536]{2,1,0:T(8,128)(2,1)} %bitcast.6, bf16[3,1536,384]{2,1,0:T(8,128)(2,1)} %bitcast.4, bf16[3,128,1536]{2,1,0:T(8,128)(2,1)} %wo_hbm.1), custom_call_target="tpu_custom_call" | custom-call | tf_op jit(solution)/shard_map/block/pallas_call | solution.py:887
  159.4 13.7 %weight_grad.1 = (f32[3,1536,384]{2,1,0:T(8,128)}, bf16[128,1536]{1,0:T(8,128)(2,1)}, f32[3,128,1536]{2,1,0:T(8,128)}) custom-call(bf16[1536,2048]{1,0:T(8,128)(2,1)} %get-tuple-element.10.x_hbm, bf16[8,256,1152]{2,1,0:T(8,128)(2,1)} %get-tuple-element.11.rows_hbm, bf16[128,1536]{1,0:T(8,128)(2,1)} %get-tuple-element.12.block_hbm, ...), custom_call_target="tpu_custom_call" | custom-call | tf_op jit(solution)/shard_map/weight_grad/pallas_call | solution.py:994

commit v6 on v5

--- a/solution.py
+++ b/solution.py
@@ -955,7 +955,7 @@
         return pltpu.make_async_copy(out.at[m % 2, :, h * 384:(h + 1) * 384], out_hbm.at[h, pl.ds(m * 256, 256)], out_sem.at[m, h])
 
     copies = [
-        pltpu.make_async_copy(rows_hbm, rows, sem.at[0]),
+        None,
         pltpu.make_async_copy(block_hbm, block_rows, sem.at[1]),
         pltpu.make_async_copy(grad_out_hbm, grad_out, sem.at[2]),
     ]
@@ -963,18 +963,32 @@
         pltpu.make_async_copy(block_rows, block_copy, sem.at[1]),
         pltpu.make_async_copy(grad_out, grad_out_copy, sem.at[2]),
     ]
-    copies[0].start()
-    for m in range(6):
+    first, rest = slice(0, 512), slice(512, 1152)
+    parts = [
+        pltpu.make_async_copy(rows_hbm.at[:, :, lanes], rows.at[:, :, lanes], sem.at[k])
+        for k, lanes in ((0, first), (3, rest))
+    ]
+    parts[0].start()
+    load(0).start()
+    parts[1].start()
+    for m in range(1, 6):
         load(m).start()
     copies[1].start()
     copies[2].start()
-    copies[0].wait()
     for m in range(6):
         load(m).wait()
         if m >= 2:
             for h in range(3):
                 store(m - 2, h).wait()
-        out[m % 2] = jnp.dot(x[m * 256:(m + 1) * 256], rows[...].reshape(2048, 1152), preferred_element_type=F32)
+        factor = x[m * 256:(m + 1) * 256]
+        if m == 0:
+            for part, lanes in zip(parts, (first, rest)):
+                part.wait()
+                out[0, :, lanes] = jnp.dot(
+                    factor, rows[:, :, lanes].reshape(2048, lanes.stop - lanes.start), preferred_element_type=F32
+                )
+        else:
+            out[m % 2] = jnp.dot(factor, rows[...].reshape(2048, 1152), preferred_element_type=F32)
         for h in range(3):
             store(m, h).start()
         if m == 1:
@@ -1007,7 +1021,7 @@
             pltpu.VMEM((2, 256, 1152), F32),
             pltpu.VMEM((128, 1536), BF16),
             pltpu.VMEM((3, 128, 1536), F32),
-            dma((6,)), dma((3,)), dma((6, 3)),
+            dma((6,)), dma((4,)), dma((6, 3)),
         ],
         compiler_params=pltpu.CompilerParams(vmem_limit_bytes=63 << 20),
     )(turned, rows, block_rows, grad_out)

time: 173 us -> 173 us (level)
  no operation moved by 1% of the time
where the time goes in v6:
time: 173 us
  Pallas kernels  172 us (99%)
    pallas_call x1, Pallas kernels, block(): pl.pallas_call(block_kernel, name='block', out_shape=(jax.ShapeDtypeStruc...  159 us
    pallas_call x1, Pallas kernels, weight_grad(): pl.pallas_call(weight_kernel, name='weight_grad', out_shape=(jax.ShapeDty...  13.2 us

profile of v6, /device:TPU:17, one launch (start us, length us, event | category | flops | bytes accessed | tf_op | source)
XLA Modules:
  0.0 172.9 jit_solution(11689580921489082085)
XLA Ops:
  0.6 158.8 %block.1 = (bf16[1536,2048]{1,0:T(8,128)(2,1)}, bf16[8,256,1152]{2,1,0:T(8,128)(2,1)}, bf16[128,1536]{1,0:T(8,128)(2,1)}, f32[3,128,1536]{2,1,0:T(8,128)}) custom-call(bf16[2,64,1536]{2,1,0:T(8,128)(2,1)} %bitcast.5, bf16[2,64,1536]{2,1,0:T(8,128)(2,1)} %bitcast.6, bf16[3,1536,384]{2,1,0:T(8,128)(2,1)} %bitcast.4, bf16[3,128,1536]{2,1,0:T(8,128)(2,1)} %wo_hbm.1), custom_call_target="tpu_custom_call" | custom-call | tf_op jit(solution)/shard_map/block/pallas_call | solution.py:887
  159.4 13.2 %weight_grad.1 = (f32[3,1536,384]{2,1,0:T(8,128)}, bf16[128,1536]{1,0:T(8,128)(2,1)}, f32[3,128,1536]{2,1,0:T(8,128)}) custom-call(bf16[1536,2048]{1,0:T(8,128)(2,1)} %get-tuple-element.10.x_hbm, bf16[8,256,1152]{2,1,0:T(8,128)(2,1)} %get-tuple-element.11.rows_hbm, bf16[128,1536]{1,0:T(8,128)(2,1)} %get-tuple-element.12.block_hbm, ...), custom_call_target="tpu_custom_call" | custom-call | tf_op jit(solution)/shard_map/weight_grad/pallas_call | solution.py:1008
